TPU v7x, 32 devices: a whole 2x2x4 slice. The times are simulated.
32 devices in a mesh: dp: 8 (over z, x), tensor: 4 (over y, core).
Axes of the slice: x: 2, y: 2, z: 4, core: 2. Of those that a mesh axis runs over, the one named last changes fastest.
Arguments:
- block_input: bfloat16 [8192, 2048], P('dp'), may hold values from -6 to 6
- out_grad: bfloat16 [8192, 2048], P('dp'), may hold values from -6 to 6
- segments: int32 [8192], P('dp'), may hold values from 0 to 3, as said below
- positions: int32 [8192], P('dp'), may hold values from 0 to 1535, as said below
- w_query: float32 [2048, 2048], P('dp', 'tensor'), may hold values from -0.1875 to 0.1875
- key_weight_master: float32 [2048, 1024], P('dp', 'tensor'), may hold values from -0.1875 to 0.1875
- value_weight_master: float32 [2048, 1024], P('dp', 'tensor'), may hold values from -0.125 to 0.125
- w_output: float32 [2048, 2048], P('tensor', 'dp'), may hold values from -0.375 to 0.375
- w_gate: float32 [2048, 8192], P('dp', 'tensor'), may hold values from -0.125 to 0.125
- w_up: float32 [2048, 8192], P('dp', 'tensor'), may hold values from -0.125 to 0.125
- w_down: float32 [8192, 2048], P('tensor', 'dp'), may hold values from -0.0625 to 0.0625
- gains: float32 [2, 2048], P(None, 'dp'), may hold values from 0.5 to 1.5
- m_query: float32 [2048, 2048], P('dp', 'tensor'), may hold values from -1024 to 1024
- first_moment_key: float32 [2048, 1024], P('dp', 'tensor'), may hold values from -1024 to 1024
- first_moment_value: float32 [2048, 1024], P('dp', 'tensor'), may hold values from -1024 to 1024
- m_output: float32 [2048, 2048], P('tensor', 'dp'), may hold values from -256 to 256
- m_gate: float32 [2048, 8192], P('dp', 'tensor'), may hold values from -160 to 160
- m_up: float32 [2048, 8192], P('dp', 'tensor'), may hold values from -160 to 160
- m_down: float32 [8192, 2048], P('tensor', 'dp'), may hold values from -320 to 320
- m_gains: float32 [2, 2048], P(None, 'dp'), may hold values from -1024 to 1024
- v_query: float32 [2048, 2048], P('dp', 'tensor'), may hold values from 32768 to 131072
- second_moment_key: float32 [2048, 1024], P('dp', 'tensor'), may hold values from 32768 to 131072
- second_moment_value: float32 [2048, 1024], P('dp', 'tensor'), may hold values from 32768 to 131072
- v_output: float32 [2048, 2048], P('tensor', 'dp'), may hold values from 2048 to 8192
- v_gate: float32 [2048, 8192], P('dp', 'tensor'), may hold values from 744 to 2730
- v_up: float32 [2048, 8192], P('dp', 'tensor'), may hold values from 744 to 2730
- v_down: float32 [8192, 2048], P('tensor', 'dp'), may hold values from 2730 to 10922
- v_gains: float32 [2, 2048], P(None, 'dp'), may hold values from 32768 to 131072
Outputs:
- block_output: bfloat16 [8192, 2048], P('dp')
- input_gradient: float32 [8192, 2048], P('dp')
- new_query: float32 [2048, 2048], P('dp', 'tensor')
- new_key: float32 [2048, 1024], P('dp', 'tensor')
- new_value: float32 [2048, 1024], P('dp', 'tensor')
- new_output: float32 [2048, 2048], P('tensor', 'dp')
- new_gate: float32 [2048, 8192], P('dp', 'tensor')
- new_up: float32 [2048, 8192], P('dp', 'tensor')
- new_down: float32 [8192, 2048], P('tensor', 'dp')
- new_gains: float32 [2, 2048], P(None, 'dp')
- new_m_query: float32 [2048, 2048], P('dp', 'tensor')
- new_m_key: float32 [2048, 1024], P('dp', 'tensor')
- new_m_value: float32 [2048, 1024], P('dp', 'tensor')
- new_m_output: float32 [2048, 2048], P('tensor', 'dp')
- new_m_gate: float32 [2048, 8192], P('dp', 'tensor')
- new_m_up: float32 [2048, 8192], P('dp', 'tensor')
- new_m_down: float32 [8192, 2048], P('tensor', 'dp')
- new_m_gains: float32 [2, 2048], P(None, 'dp')
- new_v_query: float32 [2048, 2048], P('dp', 'tensor')
- new_v_key: float32 [2048, 1024], P('dp', 'tensor')
- new_v_value: float32 [2048, 1024], P('dp', 'tensor')
- new_v_output: float32 [2048, 2048], P('tensor', 'dp')
- new_v_gate: float32 [2048, 8192], P('dp', 'tensor')
- new_v_up: float32 [2048, 8192], P('dp', 'tensor')
- new_v_down: float32 [8192, 2048], P('tensor', 'dp')
- new_v_gains: float32 [2, 2048], P(None, 'dp')
Inputs may be any that keep to these rules, and one draw needn't show every extreme that they name: `segments`: tokens 2048 * s to 2048 * s + 2047 form sequence s; within each, segment numbers start at 0, never fall, and rise by one at each document bound; each sequence holds exactly 4 documents, one of which (drawn from the seed) has exactly 1536 tokens and the others 2048 // 4 tokens together. `positions`: 0 at each document's first token and rising by one along the document.
All inputs are finite; a program needn't handle non-finite values.
Results may differ from a plain program's by a relative error of at most 0.015.
The roundings to bfloat16 on the way count: a program that leaves them out, or rounds other values in their place, can miss the bound.
Values may be sent and summed in bfloat16 or wider, within the bound.
A program may use at most 256 MiB of HBM per device.

v0:
```python
import math

import jax
import jax.numpy as jnp
from jax import lax
from jax.sharding import PartitionSpec as P

HEAD_SIZE = 128
WINDOW = 1024
STEP = 5


EPS = 1e-06
THETA = 1000000.0
BETA_ONE = 0.5
BETA_TWO = 0.5
RATE_MATRIX = 0.02
RATE_GAIN = 0.3
DECAY = 0.1
ADAM_EPS = 1e-08
NEGATIVE = -1e30


def passed_along(x, axis, by):
    devices = lax.axis_size(axis)
    pairs = [(i, i + by) for i in range(devices) if 0 <= i + by < devices]
    return lax.ppermute(x, axis, pairs)


def norm_rows(value_matrix):
    factor = lax.rsqrt(jnp.mean(value_matrix * value_matrix, -1, keepdims=True) + EPS)
    return (value_matrix * factor, factor)


def norm_back(incoming, gaussian_sample, factor, gain):
    scaled = incoming * gain
    return factor * (
        scaled - gaussian_sample * jnp.mean(scaled * gaussian_sample, -1, keepdims=True)
    )


def rotary_tables(positions):
    half = HEAD_SIZE // 2
    frequency = THETA ** (-2.0 * jnp.arange(half, dtype=jnp.float32) / HEAD_SIZE)
    angles = positions.astype(jnp.float32)[:, None] * frequency[None, :]
    cosine_table = jnp.cos(angles)
    sine_table = jnp.sin(angles)
    return (
        jnp.concatenate([cosine_table, cosine_table], -1),
        jnp.concatenate([sine_table, sine_table], -1),
    )


def apply_rotation(heads, cosine_table, sine_table):
    half = heads.shape[-1] // 2
    turned = jnp.concatenate([-heads[..., half:], heads[..., :half]], -1)
    return heads * cosine_table[:, None, :] + turned * sine_table[:, None, :]


def masked_scores(rows, key_matrix, row_segments, row_positions, key_segments, key_positions):
    scale = 1.0 / math.sqrt(HEAD_SIZE)
    scores = (
        jnp.einsum("qhgd,khd->hgqk", rows, key_matrix, preferred_element_type=jnp.float32) * scale
    )
    distance = row_positions[:, None] - key_positions[None, :]
    allowed = (
        (row_segments[:, None] == key_segments[None, :]) & (distance >= 0) & (distance < WINDOW)
    )
    return jnp.where(allowed, scores, NEGATIVE)


def attend_forward(
    query_matrix, key_matrix, value_matrix, segments, positions, key_segments, key_positions
):
    document_length = query_matrix.shape[0]
    block = min(512, document_length)

    def one_block(start):
        rows = lax.dynamic_slice_in_dim(query_matrix, start, block, 0)
        row_segments = lax.dynamic_slice_in_dim(segments, start, block, 0)
        row_positions = lax.dynamic_slice_in_dim(positions, start, block, 0)
        scores = masked_scores(
            rows, key_matrix, row_segments, row_positions, key_segments, key_positions
        )
        top = jnp.max(scores, -1, keepdims=True)
        weights = jnp.exp(scores - top)
        total = jnp.sum(weights, -1, keepdims=True)
        probs = (weights / total).astype(jnp.bfloat16)
        result = jnp.einsum(
            "hgqk,khd->qhgd", probs, value_matrix, preferred_element_type=jnp.float32
        )
        return (result.astype(jnp.bfloat16), (top + jnp.log(total))[..., 0])

    starts = jnp.arange(document_length // block, dtype=jnp.int32) * block
    results, sums = lax.map(one_block, starts)
    return (results.reshape(query_matrix.shape), sums)


def attend_backward(
    query_matrix,
    key_matrix,
    value_matrix,
    segments,
    positions,
    key_segments,
    key_positions,
    sums,
    grad_heads,
):
    document_length = query_matrix.shape[0]
    block = min(512, document_length)
    scale = 1.0 / math.sqrt(HEAD_SIZE)

    def one_block(carry, item):
        key_total, value_total = carry
        start, block_sums = item
        rows = lax.dynamic_slice_in_dim(query_matrix, start, block, 0)
        row_segments = lax.dynamic_slice_in_dim(segments, start, block, 0)
        row_positions = lax.dynamic_slice_in_dim(positions, start, block, 0)
        grad_rows = lax.dynamic_slice_in_dim(grad_heads, start, block, 0)
        scores = masked_scores(
            rows, key_matrix, row_segments, row_positions, key_segments, key_positions
        )
        probs = jnp.exp(scores - block_sums[..., None])
        value_total = value_total + jnp.einsum(
            "hgqk,qhgd->khd",
            probs.astype(jnp.bfloat16),
            grad_rows,
            preferred_element_type=jnp.float32,
        )
        prob_grad = jnp.einsum(
            "qhgd,khd->hgqk", grad_rows, value_matrix, preferred_element_type=jnp.float32
        )
        inner = jnp.sum(probs * prob_grad, -1, keepdims=True)
        score_grad = (probs * (prob_grad - inner)).astype(jnp.bfloat16)
        query_grad = (
            jnp.einsum("hgqk,khd->qhgd", score_grad, key_matrix, preferred_element_type=jnp.float32)
            * scale
        )
        key_total = (
            key_total
            + jnp.einsum("hgqk,qhgd->khd", score_grad, rows, preferred_element_type=jnp.float32)
            * scale
        )
        return ((key_total, value_total), query_grad)

    empty = jnp.zeros(key_matrix.shape, jnp.float32)
    starts = jnp.arange(document_length // block, dtype=jnp.int32) * block
    (key_grad, value_grad), query_grads = lax.scan(one_block, (empty, empty), (starts, sums))
    return (query_grads.reshape(query_matrix.shape), key_grad, value_grad)


def adamw(weight, gradient, first, second, rate, decay):
    first_new = BETA_ONE * first + (1.0 - BETA_ONE) * gradient
    second_new = BETA_TWO * second + (1.0 - BETA_TWO) * gradient * gradient
    bias_first = 1.0 - BETA_ONE**STEP
    bias_second = 1.0 - BETA_TWO**STEP
    moved = first_new / bias_first / (jnp.sqrt(second_new / bias_second) + ADAM_EPS)
    return (weight - rate * (moved + decay * weight), first_new, second_new)


def local(
    block_input,
    out_grad,
    segments,
    positions,
    w_query,
    key_weight_master,
    value_weight_master,
    w_output,
    w_gate,
    w_up,
    w_down,
    gains,
    m_query,
    first_moment_key,
    first_moment_value,
    m_output,
    m_gate,
    m_up,
    m_down,
    m_gains,
    v_query,
    second_moment_key,
    second_moment_value,
    v_output,
    v_gate,
    v_up,
    v_down,
    v_gains,
):
    tokens = block_input.shape[0]
    query_full, key_full, value_full, output_full, gain_full = (
        lax.all_gather(w_query.astype(jnp.bfloat16), "dp", axis=0, tiled=True),
        lax.all_gather(key_weight_master.astype(jnp.bfloat16), "dp", axis=0, tiled=True),
        lax.all_gather(value_weight_master.astype(jnp.bfloat16), "dp", axis=0, tiled=True),
        lax.all_gather(w_output.astype(jnp.bfloat16), "dp", axis=1, tiled=True),
        lax.all_gather(gains.astype(jnp.bfloat16), "dp", axis=1, tiled=True),
    )
    gate_full, up_full, down_full = (
        lax.all_gather(w_gate.astype(jnp.bfloat16), "dp", axis=0, tiled=True),
        lax.all_gather(w_up.astype(jnp.bfloat16), "dp", axis=0, tiled=True),
        lax.all_gather(w_down.astype(jnp.bfloat16), "dp", axis=1, tiled=True),
    )
    gain_one = gain_full[0].astype(jnp.float32)
    gain_two = gain_full[1].astype(jnp.float32)
    query_heads = query_full.shape[1] // HEAD_SIZE
    pair_heads = key_full.shape[1] // HEAD_SIZE
    head_group = query_heads // pair_heads
    inputs = block_input.astype(jnp.float32)
    normal_one, factor_one = norm_rows(inputs)
    normed_input = (normal_one * gain_one).astype(jnp.bfloat16)
    query_unrotated = jnp.dot(normed_input, query_full, preferred_element_type=jnp.float32)
    key_unrotated = jnp.dot(normed_input, key_full, preferred_element_type=jnp.float32)
    value_matrix = (
        jnp.dot(normed_input, value_full, preferred_element_type=jnp.float32)
        .astype(jnp.bfloat16)
        .reshape(tokens, pair_heads, HEAD_SIZE)
    )
    cosine_table, sine_table = rotary_tables(positions)
    query_matrix = apply_rotation(
        query_unrotated.reshape(tokens, query_heads, HEAD_SIZE), cosine_table, sine_table
    ).astype(jnp.bfloat16)
    key_matrix = apply_rotation(
        key_unrotated.reshape(tokens, pair_heads, HEAD_SIZE), cosine_table, sine_table
    ).astype(jnp.bfloat16)
    prior_keys, prior_values = passed_along((key_matrix, value_matrix), "dp", 1)
    later_half = lax.axis_index("dp") % 2 == 1
    places = jnp.arange(tokens, dtype=jnp.int32)
    first_position = positions[0]
    first_segment = segments[0]
    reached = (places >= tokens - first_position) & later_half
    prior_segments = jnp.where(reached, first_segment, -1)
    prior_positions = first_position - tokens + places
    key_rows = jnp.concatenate([prior_keys, key_matrix], 0)
    value_rows = jnp.concatenate([prior_values, value_matrix], 0)
    key_segments = jnp.concatenate([prior_segments, segments], 0)
    key_positions = jnp.concatenate([prior_positions, positions], 0)
    query_groups = query_matrix.reshape(tokens, pair_heads, head_group, HEAD_SIZE)
    attended, sums = attend_forward(
        query_groups, key_rows, value_rows, segments, positions, key_segments, key_positions
    )
    attended = attended.reshape(tokens, query_heads * HEAD_SIZE)
    mixed = lax.psum(jnp.dot(attended, output_full, preferred_element_type=jnp.float32), "tensor")
    residual = inputs + mixed
    normal_two, factor_two = norm_rows(residual)
    second_in = (normal_two * gain_two).astype(jnp.bfloat16)
    gate = jnp.dot(second_in, gate_full, preferred_element_type=jnp.float32)
    up = jnp.dot(second_in, up_full, preferred_element_type=jnp.float32)
    sigmoid = jax.nn.sigmoid(gate)
    activated = gate * sigmoid
    hidden = (activated * up).astype(jnp.bfloat16)
    branch_sum = lax.psum(
        jnp.dot(hidden, down_full, preferred_element_type=jnp.float32).astype(jnp.bfloat16),
        "tensor",
    ).astype(jnp.float32)
    block_output = (residual + branch_sum).astype(jnp.bfloat16)
    gate_back, up_back, down_back = (
        lax.all_gather(w_gate.astype(jnp.bfloat16), "dp", axis=0, tiled=True),
        lax.all_gather(w_up.astype(jnp.bfloat16), "dp", axis=0, tiled=True),
        lax.all_gather(w_down.astype(jnp.bfloat16), "dp", axis=1, tiled=True),
    )
    query_back, key_back, value_back, output_back = (
        lax.all_gather(w_query.astype(jnp.bfloat16), "dp", axis=0, tiled=True),
        lax.all_gather(key_weight_master.astype(jnp.bfloat16), "dp", axis=0, tiled=True),
        lax.all_gather(value_weight_master.astype(jnp.bfloat16), "dp", axis=0, tiled=True),
        lax.all_gather(w_output.astype(jnp.bfloat16), "dp", axis=1, tiled=True),
    )
    incoming = out_grad.astype(jnp.float32)
    grad_w_down = jnp.einsum("tf,td->fd", hidden, out_grad, preferred_element_type=jnp.float32)
    grad_hidden = jnp.einsum("td,fd->tf", out_grad, down_back, preferred_element_type=jnp.float32)
    grad_gate = (grad_hidden * up * (sigmoid + gate * sigmoid * (1.0 - sigmoid))).astype(
        jnp.bfloat16
    )
    grad_up = (grad_hidden * activated).astype(jnp.bfloat16)
    grad_w_gate = jnp.einsum("td,tf->df", second_in, grad_gate, preferred_element_type=jnp.float32)
    grad_w_up = jnp.einsum("td,tf->df", second_in, grad_up, preferred_element_type=jnp.float32)
    second_part = jnp.einsum(
        "tf,df->td", grad_gate, gate_back, preferred_element_type=jnp.float32
    ) + jnp.einsum("tf,df->td", grad_up, up_back, preferred_element_type=jnp.float32)
    grad_second = lax.psum(second_part, "tensor")
    gain_two_grad = jnp.sum(grad_second * normal_two, 0)
    residual_grad = incoming + norm_back(grad_second, normal_two, factor_two, gain_two)
    branch_grad = residual_grad.astype(jnp.bfloat16)
    grad_w_output = jnp.einsum(
        "tc,td->cd", attended, branch_grad, preferred_element_type=jnp.float32
    )
    attended_grad = jnp.einsum(
        "td,cd->tc", branch_grad, output_back, preferred_element_type=jnp.float32
    ).astype(jnp.bfloat16)
    grad_groups = attended_grad.reshape(tokens, pair_heads, head_group, HEAD_SIZE)
    query_grad, key_grad_rows, value_grad_rows = attend_backward(
        query_groups,
        key_rows,
        value_rows,
        segments,
        positions,
        key_segments,
        key_positions,
        sums,
        grad_groups,
    )
    returned_keys, returned_values = passed_along(
        (key_grad_rows[:tokens], value_grad_rows[:tokens]), "dp", -1
    )
    first_half = 1.0 - later_half.astype(jnp.float32)
    key_grad = key_grad_rows[tokens:] + first_half * returned_keys
    value_grad = value_grad_rows[tokens:] + first_half * returned_values
    query_grad = (
        apply_rotation(
            query_grad.reshape(tokens, query_heads, HEAD_SIZE), cosine_table, -sine_table
        )
        .astype(jnp.bfloat16)
        .reshape(tokens, query_heads * HEAD_SIZE)
    )
    key_grad = (
        apply_rotation(key_grad, cosine_table, -sine_table)
        .astype(jnp.bfloat16)
        .reshape(tokens, pair_heads * HEAD_SIZE)
    )
    value_grad = value_grad.reshape(tokens, pair_heads * HEAD_SIZE).astype(jnp.bfloat16)
    grad_w_query = jnp.einsum(
        "td,tc->dc", normed_input, query_grad, preferred_element_type=jnp.float32
    )
    grad_w_key = jnp.einsum("td,tc->dc", normed_input, key_grad, preferred_element_type=jnp.float32)
    grad_w_value = jnp.einsum(
        "td,tc->dc", normed_input, value_grad, preferred_element_type=jnp.float32
    )
    first_part = jnp.einsum("tc,dc->td", query_grad, query_back, preferred_element_type=jnp.float32)
    first_part = first_part + jnp.einsum(
        "tc,dc->td", key_grad, key_back, preferred_element_type=jnp.float32
    )
    first_part = first_part + jnp.einsum(
        "tc,dc->td", value_grad, value_back, preferred_element_type=jnp.float32
    )
    grad_first = lax.psum(first_part.astype(jnp.bfloat16), "tensor").astype(jnp.float32)
    gain_one_grad = jnp.sum(grad_first * normal_one, 0)
    input_gradient = residual_grad + norm_back(grad_first, normal_one, factor_one, gain_one)
    shares = (
        lax.psum_scatter(grad_w_query, "dp", scatter_dimension=0, tiled=True),
        lax.psum_scatter(grad_w_key, "dp", scatter_dimension=0, tiled=True),
        lax.psum_scatter(grad_w_value, "dp", scatter_dimension=0, tiled=True),
        lax.psum_scatter(grad_w_output, "dp", scatter_dimension=1, tiled=True),
        lax.psum_scatter(grad_w_gate, "dp", scatter_dimension=0, tiled=True),
        lax.psum_scatter(grad_w_up, "dp", scatter_dimension=0, tiled=True),
        lax.psum_scatter(grad_w_down, "dp", scatter_dimension=1, tiled=True),
        lax.psum_scatter(
            jnp.stack([gain_one_grad, gain_two_grad], 0), "dp", scatter_dimension=1, tiled=True
        ),
    )
    masters = (
        w_query,
        key_weight_master,
        value_weight_master,
        w_output,
        w_gate,
        w_up,
        w_down,
        gains,
    )
    firsts = (
        m_query,
        first_moment_key,
        first_moment_value,
        m_output,
        m_gate,
        m_up,
        m_down,
        m_gains,
    )
    seconds = (
        v_query,
        second_moment_key,
        second_moment_value,
        v_output,
        v_gate,
        v_up,
        v_down,
        v_gains,
    )
    rates = (RATE_MATRIX,) * 7 + (RATE_GAIN,)
    decays = (DECAY,) * 7 + (0.0,)
    fresh = [
        adamw(weight, gradient, first, second, rate, decay)
        for weight, gradient, first, second, rate, decay in zip(
            masters, shares, firsts, seconds, rates, decays
        )
    ]
    weights_new = [entry[0] for entry in fresh]
    firsts_new = [entry[1] for entry in fresh]
    seconds_new = [entry[2] for entry in fresh]
    return tuple([block_output, input_gradient] + weights_new + firsts_new + seconds_new)


def solution(mesh):
    return jax.shard_map(
        local,
        mesh=mesh,
        in_specs=(
            P("dp", None),
            P("dp", None),
            P("dp"),
            P("dp"),
            P("dp", "tensor"),
            P("dp", "tensor"),
            P("dp", "tensor"),
            P("tensor", "dp"),
            P("dp", "tensor"),
            P("dp", "tensor"),
            P("tensor", "dp"),
            P(None, "dp"),
            P("dp", "tensor"),
            P("dp", "tensor"),
            P("dp", "tensor"),
            P("tensor", "dp"),
            P("dp", "tensor"),
            P("dp", "tensor"),
            P("tensor", "dp"),
            P(None, "dp"),
            P("dp", "tensor"),
            P("dp", "tensor"),
            P("dp", "tensor"),
            P("tensor", "dp"),
            P("dp", "tensor"),
            P("dp", "tensor"),
            P("tensor", "dp"),
            P(None, "dp"),
        ),
        out_specs=(
            P("dp", None),
            P("dp", None),
            P("dp", "tensor"),
            P("dp", "tensor"),
            P("dp", "tensor"),
            P("tensor", "dp"),
            P("dp", "tensor"),
            P("dp", "tensor"),
            P("tensor", "dp"),
            P(None, "dp"),
            P("dp", "tensor"),
            P("dp", "tensor"),
            P("dp", "tensor"),
            P("tensor", "dp"),
            P("dp", "tensor"),
            P("dp", "tensor"),
            P("tensor", "dp"),
            P(None, "dp"),
            P("dp", "tensor"),
            P("dp", "tensor"),
            P("dp", "tensor"),
            P("tensor", "dp"),
            P("dp", "tensor"),
            P("dp", "tensor"),
            P("tensor", "dp"),
            P(None, "dp"),
        ),
        check_vma=False,
    )
```

profile of v0, /device:TPU:0, one launch (start us, length us, event | category | flops | bytes accessed | tf_op | source)
XLA Modules:
  0.0 2567.8 jit_solution(6859400082769506112)
XLA Ops:
  17.6 22.2 all_gather.31
  60.4 36.3 %all-gather.12.cloned.1.call-done = bf16[2048,256]{1,0:T(8,128)(2,1)} async-done(((bf16[256,256]{1,0:T(8,128)(2,1)}), bf16[2048,256]{1,0:T(8,128)(2,1)}) %all-gather.12.cloned.1.call-update) | async-done | bytes 1048592 | tf_op jit(solution)/shard_map/all_gather | solution.py:196
  115.9 35.3 %all-gather.8.cloned.1.call-done = bf16[2048,512]{1,0:T(8,128)(2,1)} async-done(((bf16[256,512]{1,0:T(8,128)(2,1)}), bf16[2048,512]{1,0:T(8,128)(2,1)}) %all-gather.8.cloned.1.call-update) | async-done | bytes 2097168 | tf_op jit(solution)/shard_map/all_gather | solution.py:194
  170.6 40.3 %while.27 = (s32[]{:T(128)}, bf16[2,512,2,2,128]{4,3,2,1,0:T(2,128)(2,1)}, f32[2,2,2,512]{3,2,1,0:T(2,128)S(1)}, s32[2]{0:T(128)S(1)}, s32[1024]{0:T(1024)S(1)},...) while((s32[]{:T(128)}, ...), condition=%wide.region_4.5_spmd, body=%wide.region_1.4_spmd.sunk | while | flops 2204366848 | bytes 67203336 | solution.py:95
  229.1 144.1 %all-reduce.5.cloned.1.call-done = f32[1024,2048]{1,0:T(8,128)} async-done(((f32[1024,2048]{1,0:T(8,128)}), f32[1024,2048]{1,0:T(8,128)}) %all-reduce.5.cloned.1.call-update) | async-done | bytes 8388624 | tf_op jit(solution)/shard_map/psum | solution.py:244
  385.2 115.7 %all-gather.16.cloned.1.call-done = bf16[2048,2048]{1,0:T(8,128)(2,1)} async-done(((bf16[256,2048]{1,0:T(8,128)(2,1)}), bf16[2048,2048]{1,0:T(8,128)(2,1)}) %all-gather.16.cloned.1.call-update) | async-done | bytes 8388624 | tf_op jit(solution)/shard_map/all_gather | solution.py:201
  500.9 14.9 fusion.100
  515.8 110.9 %all-gather.18.cloned.1.call-done = bf16[2048,2048]{1,0:T(8,128)(2,1)} async-done(((bf16[256,2048]{1,0:T(8,128)(2,1)}), bf16[2048,2048]{1,0:T(8,128)(2,1)}) %all-gather.18.cloned.1.call-update) | async-done | bytes 8388624 | tf_op jit(solution)/shard_map/all_gather | solution.py:202
  626.7 14.5 fusion.101
  641.2 111.7 %all-gather.20.cloned.1.call-done = bf16[2048,2048]{1,0:T(8,128)(2,1)} async-done(((bf16[2048,256]{1,0:T(8,128)(2,1)}), bf16[2048,2048]{1,0:T(8,128)(2,1)}) %all-gather.20.cloned.1.call-update) | async-done | bytes 8388624 | tf_op jit(solution)/shard_map/all_gather | solution.py:203
  752.9 21.4 multiply_convert_fusion
  774.4 12.9 fusion.102
  787.3 12.8 convolution_add_fusion
  802.1 14.6 convolution_convert_fusion
  816.7 134.6 %all-reduce.7.cloned.1.call-done = f32[1024,2048]{1,0:T(8,128)} async-done(((f32[1024,2048]{1,0:T(8,128)}), f32[1024,2048]{1,0:T(8,128)}) %all-reduce.7.cloned.1.call-update) | async-done | bytes 8388624 | tf_op jit(solution)/shard_map/psum | solution.py:281
  969.2 125.1 %while.28 = (s32[]{:T(128)}, f32[2048,2,128]{0,2,1:T(8,128)S(1)}, f32[2048,2,128]{0,2,1:T(8,128)}, f32[2,512,2,2,128]{4,1,3,2,0:T(8,128)}, s32[2]{0:T(128)S(1)},...) while((s32[]{:T(128)}, f32[2048,2,128]{0,2,1:T(8,128)S(1)}, ...), condition=%wide.region_12.13_spmd.clone, body=%wide.region_10.12_spmd.clone.sunk | while | flops 5440796672 | bytes 220287552 | solution.py:149
  983.6 13.1 fusion.187
  996.7 14.9 fusion.188
  1045.9 13.1 fusion.187
  1059.0 14.9 fusion.188
  1128.6 17.8 collective-permute-done.3
  1160.9 143.1 %all-reduce.9.cloned.1.call-done = (bf16[1024,2048]{1,0:T(8,128)(2,1)}, bf16[1024,2048]{1,0:T(8,128)(2,1)}) async-done(((bf16[1024,2048]{1,0:T(8,128)(2,1)}, bf16[1024,2048]{1,0:T(8,128)(2,1)}), (bf16[1024,2048]{1,0:T(8,128)(2,1)}, bf16[1024,2048]{1,0:T(8,128)(2,1)})) %all-reduce.9.cloned.1.call-update) | async-done | bytes 8388624 | tf_op jit(solution)/shard_map/psum | solution.py:253
  1326.3 15.5 fusion.108
  1342.0 15.3 fusion.109
  1357.4 15.3 fusion.110
  1378.0 68.8 %reduce-scatter.15.cloned.1.call-done = f32[256,256]{1,0:T(8,128)} async-done(((f32[2048,256]{1,0:T(8,128)}), f32[256,256]{1,0:T(8,128)}) %reduce-scatter.15.cloned.1.call-update) | async-done | bytes 262160 | tf_op jit(solution)/shard_map/reduce_scatter | solution.py:342
  1464.4 48.9 %reduce-scatter.25.cloned.1.call-done = f32[256,2]{1,0:T(8,128)} async-done(((f32[2048,2]{1,0:T(8,128)}), f32[256,2]{1,0:T(8,128)}) %reduce-scatter.25.cloned.1.call-update) | async-done | bytes 2064
  1515.0 89.3 %reduce-scatter.11.cloned.1.call-done = f32[256,512]{1,0:T(8,128)} async-done(((f32[2048,512]{1,0:T(8,128)}), f32[256,512]{1,0:T(8,128)}) %reduce-scatter.11.cloned.1.call-update) | async-done | bytes 524304 | tf_op jit(solution)/shard_map/reduce_scatter | solution.py:340
  1607.0 88.9 %reduce-scatter.17.cloned.1.call-done = f32[512,256]{1,0:T(8,128)} async-done(((f32[512,2048]{1,0:T(8,128)}), f32[512,256]{1,0:T(8,128)}) %reduce-scatter.17.cloned.1.call-update) | async-done | bytes 524304 | tf_op jit(solution)/shard_map/reduce_scatter | solution.py:343
  1698.7 283.9 %reduce-scatter.19.cloned.1.call-done = f32[256,2048]{1,0:T(8,128)} async-done(((f32[2048,2048]{1,0:T(8,128)}), f32[256,2048]{1,0:T(8,128)}) %reduce-scatter.19.cloned.1.call-update) | async-done | bytes 2097168 | tf_op jit(solution)/shard_map/reduce_scatter | solution.py:344
  1989.5 278.5 %reduce-scatter.21.cloned.1.call-done = f32[256,2048]{1,0:T(8,128)} async-done(((f32[2048,2048]{1,0:T(8,128)}), f32[256,2048]{1,0:T(8,128)}) %reduce-scatter.21.cloned.1.call-update) | async-done | bytes 2097168 | tf_op jit(solution)/shard_map/reduce_scatter | solution.py:345
  2275.6 278.5 %reduce-scatter.23.cloned.1.call-done = f32[2048,256]{1,0:T(8,128)} async-done(((f32[2048,2048]{1,0:T(8,128)}), f32[2048,256]{1,0:T(8,128)}) %reduce-scatter.23.cloned.1.call-update) | async-done | bytes 2097168 | tf_op jit(solution)/shard_map/reduce_scatter | solution.py:346
  (348 shorter events, 340.4 us)
Async XLA Ops:
  7.2 46.5 %all-gather.10.cloned.1.call-start = ((), (), s32[]{:S(2)}) async-start(), calls=%async_computation.9 | async-start | bytes 1179648 | tf_op jit(solution)/shard_map/all_gather | solution.py:195
  8.9 87.8 %all-gather.12.cloned.1.call-start = ((), (), s32[]{:S(2)}) async-start(), calls=%async_computation.10 | async-start | bytes 1179648 | tf_op jit(solution)/shard_map/all_gather | solution.py:196
  10.6 140.6 %all-gather.8.cloned.1.call-start = ((), (), s32[]{:S(2)}) async-start(), calls=%async_computation.8 | async-start | bytes 2359296 | tf_op jit(solution)/shard_map/all_gather | solution.py:194
  12.4 201.5 %all-gather.14.cloned.1.call-start = ((), (), s32[]{:S(2)}) async-start(), calls=%async_computation.11 | async-start | bytes 2359296 | tf_op jit(solution)/shard_map/all_gather | solution.py:197
  14.3 358.9 %all-reduce.5.cloned.1.call-start = ((), (), s32[]{:S(2)}) async-start(), calls=%async_computation.12 | async-start | bytes 16777216 | tf_op jit(solution)/shard_map/psum | solution.py:244
  57.9 47.5 %collective-permute-start = (bf16[1024,2,128]{0,2,1:T(8,128)(2,1)S(1)}, bf16[1024,2,128]{0,2,1:T(8,128)(2,1)S(1)}, u32[]{:S(2)}, u32[]{:S(2)}) collective-permute-start(bf16[1024,2,128]{0,2,1:T(8,128)(2,1)S(1)} %fusion.78), channel_id=1, source_target_pairs={{0,4},{4,8},{8,12},{12,16},{16,20},{20,24},{24,28},{1,5},{5,9},{9,... | collective-permute-start | bytes 1572872 | tf_op jit(solution)/shard_map/ppermute | solution.py:27
  100.8 15.0 collective-permute-start.1
  221.7 279.2 %all-gather.16.cloned.1.call-start = ((), (), s32[]{:S(2)}) async-start(), calls=%async_computation.13 | async-start | bytes 9437184 | tf_op jit(solution)/shard_map/all_gather | solution.py:201
  224.4 402.3 %all-gather.18.cloned.1.call-start = ((), (), s32[]{:S(2)}) async-start(), calls=%async_computation.14 | async-start | bytes 9437184 | tf_op jit(solution)/shard_map/all_gather | solution.py:202
  227.8 525.1 %all-gather.20.cloned.1.call-start = ((), (), s32[]{:S(2)}) async-start(), calls=%async_computation.15 | async-start | bytes 9437184 | tf_op jit(solution)/shard_map/all_gather | solution.py:203
  229.0 153.3 %copy-start.60 = (f32[1,2048]{1,0:T(1,128)S(1)}, f32[1,2048]{1,0:T(1,128)}, u32[]{:S(2)}) copy-start(f32[1,2048]{1,0:T(1,128)} %get-tuple-element.382) | copy-start | bytes 24580
  229.0 722.3 %all-reduce.7.cloned.1.call-start = ((), (), s32[]{:S(2)}) async-start(), calls=%async_computation.16 | async-start | bytes 16777216 | tf_op jit(solution)/shard_map/psum | solution.py:281
  800.0 503.9 %all-reduce.9.cloned.1.call-start = ((), (), s32[]{:S(2)}) async-start(), calls=%async_computation.25 | async-start | bytes 16777216 | tf_op jit(solution)/shard_map/psum | solution.py:253
  1097.1 28.3 %collective-permute-start.2 = (f32[1024,2,128]{0,2,1:T(8,128)}, f32[1024,2,128]{0,2,1:T(8,128)}, u32[]{:S(2)}, u32[]{:S(2)}) collective-permute-start(f32[1024,2,128]{0,2,1:T(8,128)} %slice.59), channel_id=1, source_target_pairs={{4,0},{8,4},{12,8},{16,12},{20,16},{24,20},{28,24},{5,1},{9,5},{13... | collective-permute-start | bytes 3145736 | tf_op jit(solution)/shard_map/ppermute | solution.py:27
  1109.5 37.0 %collective-permute-start.3 = (f32[1024,2,128]{0,2,1:T(8,128)S(1)}, f32[1024,2,128]{0,2,1:T(8,128)S(1)}, u32[]{:S(2)}, u32[]{:S(2)}) collective-permute-start(f32[1024,2,128]{0,2,1:T(8,128)S(1)} %slice.63), channel_id=1, source_target_pairs={{4,0},{8,4},{12,8},{16,12},{20,16},{24,20},{28,24},{5,1},{9,5},{13... | collective-permute-start | bytes 3145736 | tf_op jit(solution)/shard_map/ppermute | solution.py:27
  1150.1 225.9 %reduce-scatter.13.cloned.1.call-start = ((), (), s32[]{:S(2)}) async-start(), calls=%async_computation.18 | async-start | bytes 2359296 | tf_op jit(solution)/shard_map/reduce_scatter | solution.py:341
  1155.0 148.9 %copy-start.59 = (f32[1,2048]{1,0:T(1,128)S(1)}, f32[1,2048]{1,0:T(1,128)}, u32[]{:S(2)}) copy-start(f32[1,2048]{1,0:T(1,128)} %copy-done.58) | copy-start | bytes 24580
  1155.1 148.9 %copy-start.64 = (f32[1024]{0:T(1024)S(1)}, f32[1024]{0:T(1024)}, u32[]{:S(2)}) copy-start(f32[1024]{0:T(1024)} %copy-done.63) | copy-start | bytes 12292
  1155.1 291.8 %reduce-scatter.15.cloned.1.call-start = ((), (), s32[]{:S(2)}) async-start(), calls=%async_computation.19 | async-start | bytes 2359296 | tf_op jit(solution)/shard_map/reduce_scatter | solution.py:342
  1160.8 352.5 %reduce-scatter.25.cloned.1.call-start = ((), (), s32[]{:S(2)}) async-start(), calls=%async_computation.24 | async-start | bytes 1179648
  1310.4 293.8 %reduce-scatter.11.cloned.1.call-start = ((), (), s32[]{:S(2)}) async-start(), calls=%async_computation.17 | async-start | bytes 4718592 | tf_op jit(solution)/shard_map/reduce_scatter | solution.py:340
  1317.2 378.7 %reduce-scatter.17.cloned.1.call-start = ((), (), s32[]{:S(2)}) async-start(), calls=%async_computation.20 | async-start | bytes 4718592 | tf_op jit(solution)/shard_map/reduce_scatter | solution.py:343
  1326.2 656.4 %reduce-scatter.19.cloned.1.call-start = ((), (), s32[]{:S(2)}) async-start(), calls=%async_computation.21 | async-start | bytes 18874368 | tf_op jit(solution)/shard_map/reduce_scatter | solution.py:344
  1341.8 926.3 %reduce-scatter.21.cloned.1.call-start = ((), (), s32[]{:S(2)}) async-start(), calls=%async_computation.22 | async-start | bytes 18874368 | tf_op jit(solution)/shard_map/reduce_scatter | solution.py:345
  1357.3 1196.7 %reduce-scatter.23.cloned.1.call-start = ((), (), s32[]{:S(2)}) async-start(), calls=%async_computation.23 | async-start | bytes 18874368 | tf_op jit(solution)/shard_map/reduce_scatter | solution.py:346
  1372.7 74.1 %copy-start.43 = (f32[256,256]{1,0:T(8,128)S(1)}, f32[256,256]{1,0:T(8,128)}, u32[]{:S(2)}) copy-start(f32[256,256]{1,0:T(8,128)} %param.38) | copy-start | bytes 786436
  1372.7 74.1 %copy-start.52 = (f32[256,256]{1,0:T(8,128)S(1)}, f32[256,256]{1,0:T(8,128)}, u32[]{:S(2)}) copy-start(f32[256,256]{1,0:T(8,128)} %param.46) | copy-start | bytes 786436
  1372.7 74.1 %copy-start.53 = (f32[256,256]{1,0:T(8,128)S(1)}, f32[256,256]{1,0:T(8,128)}, u32[]{:S(2)}) copy-start(f32[256,256]{1,0:T(8,128)} %param.54) | copy-start | bytes 786436
  1457.3 146.9 %copy-start.32 = (f32[256,512]{1,0:T(8,128)S(1)}, f32[256,512]{1,0:T(8,128)}, u32[]{:S(2)}) copy-start(f32[256,512]{1,0:T(8,128)} %param.36) | copy-start | bytes 1572868
  1457.3 238.6 %copy-start.33 = (f32[512,256]{1,0:T(8,128)S(1)}, f32[512,256]{1,0:T(8,128)}, u32[]{:S(2)}) copy-start(f32[512,256]{1,0:T(8,128)} %param.39) | copy-start | bytes 1572868
  1464.4 518.2 %copy-start.12 = (f32[256,2048]{1,0:T(8,128)S(1)}, f32[256,2048]{1,0:T(8,128)}, u32[]{:S(2)}) copy-start(f32[256,2048]{1,0:T(8,128)} %param.40) | copy-start | bytes 6291460
  1989.5 564.5 %copy-start.14 = (f32[2048,256]{1,0:T(8,128)S(1)}, f32[2048,256]{1,0:T(8,128)}, u32[]{:S(2)}) copy-start(f32[2048,256]{1,0:T(8,128)} %param.42) | copy-start | bytes 6291460
  (78 other events, 753.8 us)
Sparse Core Ops, SparseCore 0:
  10.7 42.8 all-gather.9
  56.4 40.2 all-gather.11
  99.4 51.7 all-gather.7
  153.6 49.5 all-gather.13
  221.8 151.3 all-reduce.4
  375.8 125.0 all-gather.15
  503.6 123.1 all-gather.17
  629.3 123.5 all-gather.19
  800.2 151.0 all-reduce.6
  1150.3 153.6 all-reduce.8
  1308.1 67.9 reduce-scatter.12
  1380.0 66.7 reduce-scatter.14
  1450.8 62.4 reduce-scatter.24
  1517.3 86.9 reduce-scatter.10
  1607.7 88.1 reduce-scatter.16
  1700.1 282.5 reduce-scatter.18
  1986.3 281.7 reduce-scatter.20
  2272.2 281.8 reduce-scatter.22
where the time goes:
time: 2580 us; the launch traced here: 2570 us
  waiting for transfers between devices  2010 us (78%)
  matrix products  295 us (11%)
  other arithmetic  158 us (6%)
  local copies, waits for them, and re-layouts  49.4 us (2%)
    reduce_scatter x1, waiting for transfers between devices, local(): lax.psum_scatter(grad_w_gate, 'dp', scatter_dimension=0, tiled=True)  284 us
    reduce_scatter x1, waiting for transfers between devices, local(): lax.psum_scatter(grad_w_up, 'dp', scatter_dimension=0, tiled=True)  279 us
    reduce_scatter x1, waiting for transfers between devices, local(): lax.psum_scatter(grad_w_down, 'dp', scatter_dimension=1, tiled=True)  278 us
    psum x1, waiting for transfers between devices, local(): lax.psum(jnp.dot(attended, output_full, preferred_element_type=jnp.float3...  144 us
    psum x1, waiting for transfers between devices, local(): lax.psum(jnp.dot(hidden, down_full, preferred_element_type=jnp.float32).a...  143 us
    psum x1, waiting for transfers between devices, local(): grad_second = lax.psum(second_part, 'tensor')  135 us
    all_gather x1, waiting for transfers between devices, local(): lax.all_gather(w_gate.astype(jnp.bfloat16), 'dp', axis=0, tiled=True)  116 us
    all_gather x1, waiting for transfers between devices, local(): lax.all_gather(w_down.astype(jnp.bfloat16), 'dp', axis=1, tiled=True)  112 us
  transfers between devices with their start and end apart: 22, of which 20 were waited for; matrix products, arithmetic and copies ran while one was open for 11% of the time, Pallas kernels for 0%

commit v1 on v0

v1 whole, which is shorter than its diff:
```python
import functools
import math

import jax
import jax.numpy as jnp
from jax import lax
from jax.experimental import pallas as pl
from jax.experimental.pallas import tpu as pltpu
from jax.sharding import PartitionSpec as P

HEAD_SIZE = 128
WINDOW = 1024
STEP = 5
EPS = 1e-06
THETA = 1000000.0
BETA_ONE = 0.5
BETA_TWO = 0.5
RATE_MATRIX = 0.02
RATE_GAIN = 0.3
DECAY = 0.1
ADAM_EPS = 1e-08
NEGATIVE = -1e30
SLICES = 4
BF = jnp.bfloat16
F32 = jnp.float32
VMEM_LIMIT = 63 * 1024 * 1024
MESH = pl.DeviceIdType.MESH


class Place:
    def __init__(self, sequences):
        self.count = sequences
        self.locate()

    def locate(self):
        self.dp, self.tensor = lax.axis_index("dp"), lax.axis_index("tensor")
        self.sequence, self.half = self.dp // 2, self.dp % 2
        self.y, self.core = self.tensor // 2, self.tensor % 2
        across = 1 - 2 * self.half
        beside = 2 - 4 * self.y
        self.partner = {
            "core": (self.dp, self.tensor + 1 - 2 * self.core),
            "x": (self.dp + across, self.tensor),
            "y": (self.dp, self.tensor + beside),
            "first": (self.dp + (1 - self.core) * across, self.tensor + self.core * beside),
            "second": (self.dp + self.core * across, self.tensor + (1 - self.core) * beside),
            "right": (self.dp + 2, self.tensor),
            "left": (self.dp - 2, self.tensor),
        }

    def of_group(self, g):
        dh = (g // 4 + self.half) % 2
        dy = ((g // 2) % 2 + self.y) % 2
        dc = (g % 2 + self.core) % 2
        from_core = (self.core + dc) % 2
        straight = dh * 2 + dy
        return dc * 4 + straight + from_core * (dy * 2 + dh - straight)

    def greet(self):
        barrier = pltpu.get_barrier_semaphore()
        for name in ("core", "x", "y"):
            pl.semaphore_signal(barrier, inc=1, device_id=self.partner[name], device_id_type=MESH)

        @pl.when(self.sequence >= 1)
        def _():
            pl.semaphore_signal(barrier, inc=1, device_id=self.partner["left"], device_id_type=MESH)

        @pl.when(self.sequence <= self.count - 2)
        def _():
            pl.semaphore_signal(barrier, inc=1, device_id=self.partner["right"], device_id_type=MESH)

        ends = (self.sequence + self.count - 1) // self.count + (2 * self.count - 2 - self.sequence) // self.count
        pl.semaphore_wait(barrier, 3 + ends)

    def copy(self, source, target, send, recv, name):
        return pltpu.make_async_remote_copy(
            src_ref=source, dst_ref=target, send_sem=send, recv_sem=recv,
            device_id=self.partner[name], device_id_type=MESH,
        )


class Gather:
    moves = [("second", 0, 1), ("first", 0, 2), ("first", 1, 3)] + [("core", p, p + 4) for p in range(4)]

    def __init__(self, place, buffer, group, send, recv, own=None):
        self.place, self.buffer, self.group = place, buffer, group
        self.send, self.recv, self.own = send, recv, own

    def at(self, index):
        return self.buffer.at[pl.ds(index * self.group, self.group)]

    def copy(self, index):
        name, source, target = self.moves[index]
        source = self.own if self.own is not None and source == 0 else self.at(source)
        return self.place.copy(source, self.at(target), self.send.at[index], self.recv.at[index], name)

    def start(self):
        for index in (0, 1, 3):
            self.copy(index).start()

    def step(self, index):
        if index == 1:
            self.copy(0).wait_recv()
            self.copy(2).start()
            self.copy(4).start()
        else:
            self.copy(index - 1).wait_recv()
            self.copy(index + 3).start()

    def arrived(self, index):
        self.copy(3 + index).wait_recv()

    def sent(self):
        for index in range(7):
            self.copy(index).wait_send()


class Line:
    def __init__(self, place, slot, send, recv):
        self.place, self.slot = place, slot
        self.sends, self.recvs = send, recv

    def move(self, way, stage):
        place = self.place
        shard = place.sequence - stage if way == 0 else place.sequence + stage
        target = self.slot(shard)
        name = "right" if way == 0 else "left"
        return place.copy(target, target, self.sends.at[way, stage], self.recvs.at[way, stage], name)

    def conditions(self, stage):
        place = self.place
        last = place.count - 1
        sends = (
            (place.sequence >= stage) & (place.sequence <= last - 1),
            (place.sequence <= last - stage) & (place.sequence >= 1),
        )
        recvs = (place.sequence >= stage + 1, place.sequence <= last - 1 - stage)
        return sends, recvs

    def start(self, stage):
        for way, condition in enumerate(self.conditions(stage)[0]):
            @pl.when(condition)
            def _(way=way):
                self.move(way, stage).start()

    def arrived(self, stage):
        for way, condition in enumerate(self.conditions(stage)[1]):
            @pl.when(condition)
            def _(way=way):
                place = self.place
                shard = place.sequence - 1 - stage if way == 0 else place.sequence + 1 + stage
                target = self.slot(shard)
                place.copy(
                    target, target, self.sends.at[way, stage], self.recvs.at[way, stage],
                    "right" if way == 0 else "left",
                ).wait_recv()

    def sent(self, stage):
        for way, condition in enumerate(self.conditions(stage)[0]):
            @pl.when(condition)
            def _(way=way):
                self.move(way, stage).wait_send()


def turn(head, cosine, sine):
    return head * cosine + pltpu.roll(head, HEAD_SIZE // 2, 1) * sine


def key_range(block_at, block):
    low = max(0, block_at * block - WINDOW + 1) // block * block
    return low, (block_at + 1) * block


def allowed_pairs(segment_rows, segment_columns, block_at, block):
    low, high = key_range(block_at, block)
    shape = (block, high - low)
    distance = (
        lax.broadcasted_iota(jnp.int32, shape, 0)
        - lax.broadcasted_iota(jnp.int32, shape, 1)
        + (block_at * block - low)
    )
    same = segment_rows[block_at * block : high, 0:1] == segment_columns[0:1, low:high]
    return same & (distance >= 0) & (distance < WINDOW)


NT = (((1,), (1,)), ((), ()))
TN = (((0,), (0,)), ((), ()))


def rows_at(index, size):
    return pl.ds(pl.multiple_of(index * size, size), size)


def group_at(place, p):
    dc = p // 4
    from_core = (place.core + dc) % 2
    one, two = (p // 2) % 2, p % 2
    dh = one + from_core * (two - one)
    dy = two + from_core * (one - two)
    return ((dh + place.half) % 2) * 4 + ((dy + place.y) % 2) * 2 + (dc + place.core) % 2


def attend_blocks(place, heads, q_cols, k_cols, aux, columns_ref, between):
    block = heads.shape[0] // 8
    qkv_cols = q_cols + 2 * k_cols
    scale = 1.0 / math.sqrt(HEAD_SIZE)
    for at in range(8):
        low, high = key_range(at, block)
        allowed = allowed_pairs(aux, columns_ref, at, block)
        keys, values = heads[low:high, q_cols : q_cols + k_cols], heads[low:high, q_cols + k_cols : qkv_cols]
        to = rows_at(place.of_group(at), block)
        for head in range(q_cols // HEAD_SIZE):
            columns = slice(head * HEAD_SIZE, (head + 1) * HEAD_SIZE)
            rows = heads[at * block : high, columns]
            scores = lax.dot_general(rows, keys, NT, preferred_element_type=F32) * scale
            scores = jnp.where(allowed, scores, NEGATIVE)
            top = jnp.max(scores, -1, keepdims=True)
            weights = jnp.exp(scores - top)
            total = jnp.sum(weights, -1, keepdims=True)
            probs = (weights * (1.0 / total)).astype(BF)
            heads[to, qkv_cols + columns.start : qkv_cols + columns.stop] = jnp.dot(
                probs, values, preferred_element_type=F32
            ).astype(BF)
            aux[at * block : high, 1 + head : 2 + head] = top + jnp.log(total)
        between(at)


class LineSum:
    def __init__(self, place, item, rows, index, own, recv, loads, ring, send_sem, recv_sem, load_sem, before):
        self.place, self.item, self.index, self.own, self.recv = place, item, index, own, recv
        self.rows = pl.ds(*rows)
        self.loads, self.ring = loads.at[:, self.rows], ring.at[:, self.rows]
        self.send_sem, self.recv_sem, self.load_sem = send_sem, recv_sem, load_sem
        self.before = before
        self.width = recv.shape[-1]

    def own_part(self, d):
        return self.own.at[self.item, self.rows, pl.ds(pl.multiple_of(d * self.width, self.width), self.width)]

    def dest(self, way, j):
        return self.place.count - 1 - j if way == 0 else j

    def move(self, way, j, source):
        return self.place.copy(
            source, self.recv.at[self.item, way, j, self.rows],
            self.send_sem.at[self.index, way, j], self.recv_sem.at[self.index, way, j],
            "right" if way == 0 else "left",
        )

    def start(self):
        last = self.place.count - 1
        for way, end in ((0, 0), (1, last)):
            @pl.when(self.place.sequence == end)
            def _(way=way):
                for j in range(last):
                    self.move(way, j, self.own_part(self.dest(way, j))).start()

    def turn_of(self, way, stage):
        depth = self.place.sequence if way == 0 else self.place.count - 1 - self.place.sequence
        return (depth >= 1) & (depth <= stage - 1), stage - 1 - depth, depth

    def slot(self, way, j):
        return j if way == 0 else self.place.count - 1 - self.place.sequence + j

    def own_load(self, way, d):
        return pltpu.make_async_copy(self.own_part(d), self.loads.at[2 * way], self.load_sem.at[2 * way])

    def came_load(self, way, j):
        return pltpu.make_async_copy(
            self.recv.at[self.item, way, j, self.rows], self.loads.at[2 * way + 1], self.load_sem.at[2 * way + 1]
        )

    def prepare(self, stage):
        for way in (0, 1):
            condition, j, _ = self.turn_of(way, stage)

            @pl.when(condition)
            def _(way=way, j=j):
                self.own_load(way, self.dest(way, j)).start()
                self.move(way, j, self.ring.at[self.slot(way, j)]).wait_recv()
                self.came_load(way, j).start()

    def service(self, stage):
        for way in (0, 1):
            condition, j, _ = self.turn_of(way, stage)

            @pl.when(condition)
            def _(way=way, j=j):
                slot = self.slot(way, j)
                if self.before is not None:
                    self.before.move(way, j, self.before.ring.at[slot]).wait_send()
                self.own_load(way, self.dest(way, j)).wait()
                self.came_load(way, j).wait()
                self.ring[slot] = (self.loads[2 * way].astype(F32) + self.loads[2 * way + 1].astype(F32)).astype(BF)
                self.move(way, j, self.ring.at[slot]).start()

    def last(self, way):
        place = self.place
        if way == 0:
            return place.sequence >= 1, place.count - 1 - place.sequence
        return place.sequence <= place.count - 2, place.sequence

    def prepare_total(self):
        self.own_load(0, self.place.sequence).start()
        for way in (0, 1):
            condition, j = self.last(way)

            @pl.when(condition)
            def _(way=way, j=j):
                self.move(way, j, self.loads.at[2 * way + 1]).wait_recv()
                self.came_load(way, j).start()

            @pl.when(jnp.logical_not(condition))
            def _(way=way):
                self.loads[2 * way + 1] = jnp.zeros(self.loads.shape[1:], BF)

    def total(self, out):
        self.own_load(0, self.place.sequence).wait()
        for way in (0, 1):
            condition, j = self.last(way)

            @pl.when(condition)
            def _(way=way, j=j):
                self.came_load(way, j).wait()

        out[...] = (
            self.loads[0].astype(F32) + self.loads[1].astype(F32) + self.loads[3].astype(F32)
        ).astype(BF)

    def sent(self, last_item):
        last = self.place.count - 1
        for way, end in ((0, 0), (1, last)):
            @pl.when(self.place.sequence == end)
            def _(way=way):
                for j in range(last):
                    self.move(way, j, self.own_part(self.dest(way, j))).wait_send()

        if last_item:
            for stage in range(2, last + 1):
                for way in (0, 1):
                    condition, j, _ = self.turn_of(way, stage)

                    @pl.when(condition)
                    def _(way=way, j=j):
                        self.move(way, j, self.ring.at[self.slot(way, j)]).wait_send()


class PlaneSum:
    def __init__(self, place, part, own, got, send_sem, recv_sem, chunk):
        self.place, self.part, self.own, self.got = place, part, own, got
        self.send_sem, self.recv_sem, self.chunk = send_sem, recv_sem, chunk
        self.group = own.shape[0]

    def columns(self, c):
        return pl.ds(c * self.chunk, self.chunk)

    def move(self, step, c):
        group, columns = self.group, self.columns(c)
        rows = ((4, 4), (2, 2), (1, 1))[step]
        name = ("core", "first", "second")[step]
        return self.place.copy(
            self.part.at[pl.ds(rows[0] * group, rows[1] * group), columns], self.got[step].at[:, columns],
            self.send_sem.at[step, c], self.recv_sem.at[step, c], name,
        )

    def push(self, c):
        self.move(0, c).start()

    def middle(self, c):
        self.move(0, c).wait_recv()
        rows, columns = pl.ds(2 * self.group, 2 * self.group), self.columns(c)
        self.part[rows, columns] = (
            self.part[rows, columns].astype(F32) + self.got[0][rows, columns].astype(F32)
        ).astype(BF)
        self.move(1, c).start()

    def late(self, c):
        self.move(1, c).wait_recv()
        rows, columns = pl.ds(self.group, self.group), self.columns(c)
        self.part[rows, columns] = (
            self.part[rows, columns].astype(F32)
            + self.got[0][rows, columns].astype(F32)
            + self.got[1][rows, columns].astype(F32)
        ).astype(BF)
        self.move(2, c).start()

    def total(self, c):
        self.move(2, c).wait_recv()
        rows, columns = pl.ds(0, self.group), self.columns(c)
        self.own[:, columns] = (
            self.own[:, columns]
            + self.got[0][rows, columns].astype(F32)
            + self.got[1][rows, columns].astype(F32)
            + self.got[2][:, columns].astype(F32)
        )

    def sent(self, c):
        for step in range(3):
            self.move(step, c).wait_send()


class HalfGather:
    def __init__(self, place, own, buffer, send, recv, local):
        self.place = place
        group = own.shape[0]
        tensor, across = place.tensor, place.tensor + 2 - 4 * place.y

        def at(index):
            return buffer.at[rows_at(index, group)]

        self.keep = pltpu.make_async_copy(own, at(tensor), local)
        self.y = place.copy(own, at(tensor), send.at[0], recv.at[0], "y")
        self.core = place.copy(own, at(tensor), send.at[1], recv.at[1], "core")
        self.far = place.copy(at(across), at(across), send.at[2], recv.at[2], "core")

    def start(self):
        self.keep.start()
        self.y.start()
        self.core.start()

    def step(self):
        self.y.wait_recv()
        self.far.start()

    def end(self):
        self.keep.wait()
        self.y.wait_send()
        self.core.wait()
        self.far.wait()


def layer_kernel(
    count, gains_here,
    block_input, out_grad, gains, table_half, marks_half,
    w_query, w_key, w_value, w_output, w_gate, w_up, w_down,
    block_output, input_gradient, shares, gain_out,
    own_grads, line_got, w_attention, w_forward, normed_out, heads_out, table_out, aux_out,
    second, grad, both, wide, got_core, got_first, got_second, loads, ring, ready, turned,
    one, two, own_rows, small_own, small_got, small_all, gain_ref, marks_ref,
    load_sem, wide_sem, ready_sem, swap_send, swap_recv, line_send, line_recv, sum_send, sum_recv,
    gather_send, gather_recv, half_send, half_recv, small_send, small_recv, gain_send, gain_recv, free_sem,
    line_load_sem, early_send, early_recv, slice_send, slice_recv, shard_send, shard_recv, master_sem, keep_sem, out_sem,
):
    place = Place(count)
    group, width = own_rows.shape
    tokens = 8 * group
    packed = wide.shape[1]
    slice_cols = packed // 3
    pair = 2 * slice_cols
    shard = w_query.shape[0]
    q_cols, k_cols = w_query.shape[1] // 2, w_key.shape[1] // 2
    qkv_cols = q_cols + 2 * k_cols
    shard2 = line_got.shape[-1]
    part_width = shares.shape[-1]
    chunk = width // 8
    big = width // 4
    block = 2 * group
    got = (got_core, got_first, got_second)

    def load_wide(source, index):
        return pltpu.make_async_copy(source, wide, wide_sem.at[index])

    def shard_rows():
        return pl.ds(pl.multiple_of(place.dp * shard, shard), shard)

    def sequence_rows(k):
        return pl.ds(pl.multiple_of(k * 2 * shard, 2 * shard), 2 * shard)

    local = pltpu.make_async_copy

    masters = [
        local(w_query, one.at[pl.ds(0, shard), pl.ds(0, 2 * q_cols)], master_sem.at[0]),
        local(w_key, one.at[pl.ds(0, shard), pl.ds(2 * q_cols, 2 * k_cols)], master_sem.at[1]),
        local(w_value, one.at[pl.ds(0, shard), pl.ds(2 * q_cols + 2 * k_cols, 2 * k_cols)], master_sem.at[2]),
    ]
    own_loads = [
        local(block_input.at[rows_at(place.tensor, group)], both.at[pl.ds(0, group)], load_sem.at[2]),
        local(out_grad.at[rows_at(place.tensor, group)], grad.at[pl.ds(0, group)], load_sem.at[3]),
    ]
    table_keep = local(table_half, table_out.at[rows_at(place.half, 4 * group)], load_sem.at[4])
    for copy in masters + own_loads + [table_keep]:
        copy.start()
    marks_ref[:, rows_at(place.half, 4 * group)] = marks_half[...]

    def early(index):
        columns = rows_at(place.half, 4 * group)
        source, target = (
            (own_rows.at[pl.ds(0, shard), pl.ds(0, packed)], wide.at[shard_rows()]),
            (marks_half, marks_ref.at[:, columns]),
            (table_half, table_out.at[columns]),
            (gains, gain_ref.at[:, shard_rows()] if gains_here else None),
        )[index]
        return place.copy(source, target, early_send.at[index], early_recv.at[index], "x")

    def unit(s, theirs, part):
        k = 2 * s + theirs
        if part == 0:
            return pl.ds((k // 4) * slice_cols, shard), pl.ds((k % 4) * pair, pair)
        return pl.ds(pair, shard), pl.ds(k * slice_cols, slice_cols)

    def slice_target(s, part):
        return w_forward.at[s, shard_rows(), pl.ds(0, pair) if part == 0 else pl.ds(pair, slice_cols)]

    def slice_swap(s, part):
        return place.copy(
            turned.at[unit(s, 1, part)], slice_target(s, part), slice_send.at[s, part], slice_recv.at[s, part], "x"
        )

    def slice_keep(s, part):
        return local(turned.at[unit(s, 0, part)], slice_target(s, part), keep_sem.at[s, part])

    lines = [
        Line(
            place, lambda k: wide.at[sequence_rows(k), pl.ds(0, qkv_cols)], shard_send.at[0], shard_recv.at[0]
        )
    ] + [
        Line(
            place, lambda k, s=s: w_forward.at[s, sequence_rows(k)], shard_send.at[1 + s], shard_recv.at[1 + s]
        )
        for s in range(SLICES)
    ]
    output_line = Line(
        place, lambda k: wide.at[sequence_rows(k), pl.ds(qkv_cols, q_cols)],
        shard_send.at[2 + SLICES], shard_recv.at[2 + SLICES],
    )

    def output_steps(first, last):
        for stage in range(min(first, count - 1), min(last, count - 1)):
            output_line.arrived(stage)
            if stage < count - 2:
                output_line.start(stage + 1)

    gain_shards = Line(
        place, lambda k: gain_ref.at[:, sequence_rows(k)], shard_send.at[1 + SLICES], shard_recv.at[1 + SLICES]
    )

    begin = (0, 1, 2 * count - 3, 3 * count - 4)
    sends = sorted(
        ((s, stage) for s in range(SLICES) for stage in range(count - 1)),
        key=lambda item: (begin[item[0]] + 2 * item[1], item[0]),
    )

    def advance(number):
        for _ in range(min(number, len(sends))):
            s, stage = sends.pop(0)
            if stage == 0:
                for part in range(2):
                    slice_swap(s, part).wait_recv()
            else:
                lines[1 + s].arrived(stage - 1)
            lines[1 + s].start(stage)

    def advance_through(s):
        while any(item[0] == s for item in sends):
            advance(1)

    place.greet()

    def attention_shard(output, target, rows, side):
        target[rows, :q_cols] = one[:shard, rows_at(side, q_cols)].astype(BF)
        for index in range(2):
            base = 2 * q_cols + 2 * k_cols * index
            target[rows, q_cols + k_cols * index : q_cols + k_cols * (index + 1)] = one[
                :shard, pl.ds(pl.multiple_of(base + side * k_cols, k_cols), k_cols)
            ].astype(BF)
        target[rows, qkv_cols:packed] = output[rows_at(side, q_cols), :].T.astype(BF)

    def fill_attention(output):
        place.locate()
        output_load = local(w_output, output, master_sem.at[3])
        output_load.start()
        for copy in masters + [output_load]:
            copy.wait()
        attention_shard(output, own_rows, slice(0, shard), 1 - place.half)
        early(0).start()
        attention_shard(output, wide, shard_rows(), place.half)

    pl.run_scoped(fill_attention, pltpu.VMEM(w_output.shape, F32))
    place.locate()
    masters = [
        local(w_gate, one.at[pl.ds(0, shard)], master_sem.at[0]),
        local(w_up, two.at[pl.ds(0, shard)], master_sem.at[1]),
    ]
    for copy in masters:
        copy.start()
    early(1).start()
    if gains_here:
        gain_ref[:, shard_rows()] = gains[...]
        early(3).start()
    else:
        gain_ref[...] = gains[...]
    inputs = Gather(place, both, group, gather_send.at[0], gather_recv.at[0])
    own_loads[0].wait()
    inputs.start()
    early(0).wait_recv()
    lines[0].start(0)
    if gains_here:
        early(3).wait_recv()
        gain_shards.start(0)

    def fill_slices(down):
        place.locate()
        down_load = local(w_down, down, master_sem.at[2])
        down_load.start()
        for copy in masters + [down_load]:
            copy.wait()
        for s in range(SLICES):
            for theirs in (1, 0):
                side = place.half + theirs - 2 * theirs * place.half
                columns = rows_at(side * SLICES + s, slice_cols)
                (rows, at), (down_rows, down_at) = unit(s, theirs, 0), unit(s, theirs, 1)
                turned[rows, pl.ds(at.start, slice_cols)] = one[:shard, columns].astype(BF)
                turned[rows, pl.ds(at.start + slice_cols, slice_cols)] = two[:shard, columns].astype(BF)
                turned[down_rows, down_at] = down[columns, :].T.astype(BF)
            for part in range(2):
                slice_keep(s, part).start()
            if s == 0:
                inputs.step(1)

    pl.run_scoped(fill_slices, pltpu.VMEM(w_down.shape, F32))
    place.locate()
    if gains_here:
        for stage in range(count - 1):
            gain_shards.arrived(stage)
            if stage < count - 2:
                gain_shards.start(stage + 1)
    lines[0].arrived(0)
    if count > 2:
        lines[0].start(1)

    def start_swap(s):
        for part in range(2):
            slice_swap(s, part).start()

    inputs.step(2)
    inputs.step(3)
    start_swap(0)
    start_swap(1)
    early(2).start()

    def norm_block(p, _):
        rows = rows_at(p, group)
        x = both[rows, :].astype(F32)
        factor = lax.rsqrt(jnp.mean(x * x, -1, keepdims=True) + EPS)
        second[rows, :] = (x * factor * gain_ref[0:1, :]).astype(BF)
        return 0

    lax.fori_loop(0, 4, norm_block, 0)
    for stage in range(1, count - 1):
        lines[0].arrived(stage)
        if stage < count - 2:
            lines[0].start(stage + 1)
    for p in range(4):
        inputs.arrived(p)
    lax.fori_loop(4, 8, norm_block, 0)
    for s in range(SLICES):
        for part in range(2):
            slice_keep(s, part).wait()
    output_line.start(0)
    grads = Gather(place, grad, group, gather_send.at[2], gather_recv.at[2])
    own_loads[1].wait()
    grads.start()
    start_swap(2)
    normed_copy = local(second, normed_out, out_sem.at[0])
    wide_copy = local(wide, w_attention, out_sem.at[1])
    normed_copy.start()
    mixed = PlaneSum(place, both, two, got, sum_send.at[0], sum_recv.at[0], chunk)

    def attention_forward(heads, table, aux):
        place.locate()
        table_keep.wait()
        early(2).wait_recv()
        table_load = local(table_out, table, load_sem.at[4])
        table_load.start()
        aux[...] = jnp.zeros_like(aux)
        early(1).wait_recv()
        tile = (HEAD_SIZE, HEAD_SIZE)
        diagonal = lax.broadcasted_iota(jnp.int32, tile, 0) == lax.broadcasted_iota(jnp.int32, tile, 1)
        for at in range(0, tokens, HEAD_SIZE):
            aux[at : at + HEAD_SIZE, 0:1] = jnp.sum(
                jnp.where(diagonal, marks_ref[0:1, at : at + HEAD_SIZE], 0.0), -1, keepdims=True
            )
        table_load.wait()

        def project_block(p, _):
            out = jnp.dot(second[rows_at(p, group), :], wide[:, :qkv_cols], preferred_element_type=F32)
            to = rows_at(group_at(place, p), group)
            cosine, sine = rotation(table[to, :])
            for at in range(0, q_cols + k_cols, HEAD_SIZE):
                heads[to, at : at + HEAD_SIZE] = turn(out[:, at : at + HEAD_SIZE], cosine, sine).astype(BF)
            heads[to, q_cols + k_cols : qkv_cols] = out[:, q_cols + k_cols :].astype(BF)
            return 0

        lax.fori_loop(0, 8, project_block, 0)
        output_steps(0, 1)
        advance(1)
        grads.step(1)

        def between(at):
            if at == 2:
                output_steps(1, 2)
            if at == 3:
                advance(1)
            if at == 5:
                output_steps(2, count)
            if at == 6:
                advance(1)

        attend_blocks(place, heads, q_cols, k_cols, aux, marks_ref, between)
        wide_copy.start()
        heads_copy = local(heads, heads_out, out_sem.at[2])
        aux_copy = local(aux, aux_out, out_sem.at[3])
        heads_copy.start()
        aux_copy.start()
        inputs.sent()
        normed_copy.wait()

        for c in range(8):
            columns = pl.ds(c * chunk, chunk)

            def mixed_part(rows, c=c):
                return lax.dot_general(
                    heads[rows, qkv_cols:], wide[c * chunk : (c + 1) * chunk, qkv_cols:], NT,
                    preferred_element_type=F32,
                )

            def mixed_rows(b, _, columns=columns, mixed_part=mixed_part):
                rows = rows_at(b, block)
                both[rows, columns] = mixed_part(rows).astype(BF)
                return 0

            first = mixed_part(pl.ds(0, block))
            two[:, columns] = first[:group]
            both[pl.ds(group, group), columns] = first[group:].astype(BF)
            lax.fori_loop(1, 4, mixed_rows, 0)
            mixed.push(c)
            if c >= 1:
                mixed.middle(c - 1)
            if c >= 3:
                mixed.late(c - 3)
            if c >= 5:
                mixed.total(c - 5)
            if c == 2:
                advance(1)
            if c == 3:
                grads.step(2)
            if c == 4:
                grads.step(3)
            if c == 6:
                advance(1)
        heads_copy.wait()
        aux_copy.wait()

    pl.run_scoped(
        attention_forward,
        pltpu.VMEM((tokens, packed), BF), pltpu.VMEM((tokens, HEAD_SIZE), F32), pltpu.VMEM((tokens, HEAD_SIZE), F32),
    )
    place.locate()
    mixed.middle(7)
    for c in (5, 6, 7):
        mixed.late(c)
        mixed.total(c - 2)
    mixed.total(6)
    mixed.total(7)
    early(0).wait_send()

    def by_rows(step):
        def some(b, _):
            step(rows_at(b, group // 4))
            return 0

        lax.fori_loop(0, 4, some, 0)

    def residual_step(rows):
        residual = two[rows, :] + both[rows, :].astype(F32)
        two[rows, :] = residual
        factor = lax.rsqrt(jnp.mean(residual * residual, -1, keepdims=True) + EPS)
        normal = (residual * factor * gain_ref[1:2, :]).astype(BF)
        own_rows[rows, :] = normal
        second[rows, :] = normal

    by_rows(residual_step)
    seconds = Gather(place, second, group, gather_send.at[1], gather_recv.at[1], own_rows)
    seconds.start()
    start_swap(3)
    advance(1)
    seconds.step(1)
    advance(1)
    wide_copy.wait()
    for stage in range(count - 1):
        lines[0].sent(stage)
        output_line.sent(stage)
    for c in range(8):
        mixed.sent(c)
    for s in range(SLICES):
        for part in range(2):
            if s < SLICES - 1:
                slice_swap(s, part).wait_send()
    seconds.step(2)
    seconds.step(3)
    for part in range(2):
        slice_swap(SLICES - 1, part).wait_send()
    for p in range(4):
        grads.arrived(p)
    advance(1)
    for p in range(4):
        seconds.arrived(p)
    seconds.sent()
    grads.sent()

    sums = []
    sum_items = [(s, 0, packed) for s in range(SLICES)]
    sum_items += [(SLICES, qkv_cols, q_cols), (SLICES, 0, qkv_cols)]
    for index, (item, low, size) in enumerate(sum_items):
        sums.append(
            LineSum(
                place, item, (low, size), index, own_grads, line_got, loads, ring, line_send, line_recv, line_load_sem,
                sums[-1] if sums else None,
            )
        )

    pending = {0: [], 1: []}
    turn_at = [0]

    def next_ready():
        slot = turn_at[0] % 2
        turn_at[0] += 1
        for wait in pending[slot]:
            wait()
        pending[slot] = []
        return slot

    def flush():
        for slot in (0, 1):
            for wait in pending[slot]:
                wait()
            pending[slot] = []

    swaps = []

    def finish(index):
        item, low, size = sum_items[index]
        slot = next_ready()
        rows = pl.ds(low, size)
        sums[index].total(ready.at[slot, rows, pl.ds(0, shard2)])

        def parts():
            if part_width == shard2:
                mine = theirs = ready.at[slot, rows, pl.ds(0, shard2)]
            else:
                mine, theirs = [
                    ready.at[slot, rows, pl.ds(pl.multiple_of(side * part_width, part_width), part_width)]
                    for side in (place.half, 1 - place.half)
                ]
            target = shares.at[place.half, item, rows]
            keep = pltpu.make_async_copy(mine, target, ready_sem.at[slot])
            swap = place.copy(theirs, target, swap_send.at[index], swap_recv.at[index], "x")
            return keep, swap

        for copy in parts():
            copy.start()
        pending[slot] += [lambda: parts()[0].wait(), lambda: parts()[1].wait_send()]
        swaps.append(lambda: parts()[1].wait_recv())

    def stages_of(kind):
        return list(range(2, min(3, count)) if kind == "first" else range(3, count))

    def prepare(item, kind):
        if kind == "total":
            sums[item].prepare_total()
        elif stages_of(kind):
            sums[item].prepare(stages_of(kind)[0])

    def complete(item, kind):
        if kind == "total":
            finish(item)
            return
        for index, stage in enumerate(stages_of(kind)):
            if index:
                sums[item].prepare(stage)
            sums[item].service(stage)

    def weight_grads(item, low, high, right, tasks=()):
        for c in range(4):
            for at, do, task in tasks:
                if at == c:
                    do(*task)
            slot = next_ready()
            columns = pl.ds(c * big, big)
            for first, last, matrix in zip(low, high, right):
                ready[slot, first:last, :] = jnp.dot(
                    turned[first:last, :], matrix[:, columns], preferred_element_type=F32
                ).astype(BF)
            rows = pl.ds(low[0], high[-1] - low[0])
            copy = pltpu.make_async_copy(ready.at[slot, rows], own_grads.at[item, rows, columns], ready_sem.at[slot])
            copy.start()
            pending[slot].append(copy.wait)

    plane = PlaneSum(place, grad, one, got, sum_send.at[1], sum_recv.at[1], chunk)

    def give_credit(index):
        for name in ("core", "first", "second"):
            pl.semaphore_signal(free_sem.at[index], inc=1, device_id=place.partner[name], device_id_type=MESH)

    def second_step(rows):
        residual, grad_second = two[rows, :], one[rows, :]
        factor = lax.rsqrt(jnp.mean(residual * residual, -1, keepdims=True) + EPS)
        normal = residual * factor
        small_own[1:2, :] += jnp.sum(grad_second * normal, 0, keepdims=True)
        scaled = grad_second * gain_ref[1:2, :]
        residual_grad = grad[rows, :].astype(F32) + factor * (
            scaled - normal * jnp.mean(scaled * normal, -1, keepdims=True)
        )
        one[rows, :] = residual_grad
        own_rows[rows, :] = residual_grad.astype(BF)
        both[rows, :] = residual_grad.astype(BF)

    branch = Gather(place, both, group, gather_send.at[3], gather_recv.at[3], own_rows)

    def feed_forward(hidden):
        place.locate()
        for s in range(SLICES):
            advance_through(s)
            lines[1 + s].arrived(count - 2)
            load_wide(w_forward.at[s], s).start()
            load_wide(w_forward.at[s], s).wait()

            def rows_step(b, _, s=s):
                rows = rows_at(b, block)
                gate_up = jnp.dot(second[rows, :], wide[:, :pair], preferred_element_type=F32)
                grad_hidden = jnp.dot(grad[rows, :], wide[:, pair:], preferred_element_type=F32)
                gate, up = gate_up[:, :slice_cols], gate_up[:, slice_cols:]
                sigmoid = 1.0 / (1.0 + jnp.exp(-gate))
                activated = gate * sigmoid
                hidden_rows = (activated * up).astype(BF)
                gate_rows = (grad_hidden * up * (sigmoid + activated * (1.0 - sigmoid))).astype(BF)
                up_rows = (grad_hidden * activated).astype(BF)
                hidden[rows, s * slice_cols : (s + 1) * slice_cols] = hidden_rows
                both[rows, s * pair : s * pair + slice_cols] = gate_rows
                both[rows, s * pair + slice_cols : (s + 1) * pair] = up_rows
                turned[:slice_cols, rows] = gate_rows.T
                turned[slice_cols:pair, rows] = up_rows.T
                turned[pair:, rows] = hidden_rows.T
                return 0

            lax.fori_loop(0, 4, rows_step, 0)
            advance(1)
            weight_grads(
                s, (0, pair), (pair, packed), (second, grad),
                (
                    (),
                    ((2, prepare, (0, "first")), (3, complete, (0, "first"))),
                    ((2, prepare, (0, "later")), (3, complete, (0, "later"))),
                    (
                        (0, prepare, (0, "total")), (1, complete, (0, "total")),
                        (2, prepare, (1, "first")), (3, complete, (1, "first")),
                    ),
                )[s],
            )
            flush()
            sums[s].start()
            advance(1)

        def chunk_loads(c, low):
            base = (c % 2) * SLICES
            return [
                pltpu.make_async_copy(
                    w_forward.at[s, pl.ds(c * chunk, chunk), pl.ds(low, packed - low)],
                    wide.at[pl.ds((base + s) * chunk, chunk), pl.ds(low, packed - low)],
                    wide_sem.at[SLICES + base + s],
                )
                for s in range(SLICES)
            ]

        def summed(source, rows, step, low, high, base):
            return sum(
                lax.dot_general(
                    source[rows, s * step : (s + 1) * step],
                    wide[(base + s) * chunk : (base + s + 1) * chunk, low:high], NT,
                    preferred_element_type=F32,
                )
                for s in range(SLICES)
            )

        for copy in chunk_loads(0, 0):
            copy.start()
        for c in range(8):
            if c < 7:
                for copy in chunk_loads(c + 1, 0):
                    copy.start()
            for copy in chunk_loads(c, 0):
                copy.wait()
            base = (c % 2) * SLICES
            columns = pl.ds(c * chunk, chunk)

            def grad_rows(b, _, columns=columns, base=base):
                rows = rows_at(b, block)
                grad[rows, columns] = summed(both, rows, pair, 0, pair, base).astype(BF)
                return 0

            first = summed(both, pl.ds(0, block), pair, 0, pair, base)
            one[:, columns] = first[:group]
            grad[pl.ds(group, group), columns] = first[group:].astype(BF)
            lax.fori_loop(1, 4, grad_rows, 0)
            plane.push(c)
            if c >= 1:
                plane.middle(c - 1)
            if c >= 2:
                plane.late(c - 2)
            if c >= 3:
                plane.total(c - 3)
            if c == 3:
                prepare(1, "later")
            if c == 4:
                complete(1, "later")
        for copy in chunk_loads(0, pair):
            copy.start()
        plane.middle(7)
        plane.late(6)
        plane.late(7)
        prepare(1, "total")
        for c in (5, 6, 7):
            plane.total(c)
        give_credit(0)
        complete(1, "total")
        small_own[...] = jnp.zeros_like(small_own)
        by_rows(second_step)
        branch.start()
        prepare(2, "first")
        for c in range(8):
            if c < 7:
                for copy in chunk_loads(c + 1, pair):
                    copy.start()
            for copy in chunk_loads(c, pair):
                copy.wait()

            def branch_rows(b, _, c=c):
                rows = rows_at(b, block)
                second[rows, pl.ds(c * chunk, chunk)] = summed(
                    hidden, rows, slice_cols, pair, packed, (c % 2) * SLICES
                ).astype(BF)
                return 0

            lax.fori_loop(0, 4, branch_rows, 0)
            if c == 0:
                complete(2, "first")
            if c == 5:
                branch.step(1)

    pl.run_scoped(feed_forward, pltpu.VMEM((tokens, SLICES * slice_cols), BF))
    place.locate()
    w_load = load_wide(w_attention, 0)
    w_load.start()

    outer = PlaneSum(place, second, two, got, sum_send.at[2], sum_recv.at[2], width)

    def rows_add(target, first_row, rows, sources):
        def step(b, _):
            at = rows_at(b, group)
            to = pl.ds(pl.multiple_of(first_row + b * group, group), group)
            value = target[to, :].astype(F32)
            for source in sources:
                value = value + source[to, :].astype(F32)
            target[to, :] = value.astype(BF)
            return 0

        lax.fori_loop(0, rows // group, step, 0)

    pl.semaphore_wait(free_sem.at[0], 3)
    outer.push(0)
    for c in range(8):
        plane.sent(c)
    marks = [0, q_cols, q_cols + k_cols, qkv_cols, qkv_cols + q_cols, qkv_cols + 2 * q_cols]
    arrays = [local(heads_out, grad.at[:, pl.ds(0, packed)], load_sem.at[5])]
    for copy in arrays:
        copy.start()
    q_ref, k_ref = grad.at[:, pl.ds(0, q_cols)], grad.at[:, pl.ds(marks[1], k_cols)]
    v_ref, attended = grad.at[:, pl.ds(marks[2], k_cols)], grad.at[:, pl.ds(marks[3], q_cols)]
    attended_grad, qkv_grad = grad.at[:, pl.ds(marks[4], q_cols)], grad.at[:, pl.ds(marks[5], qkv_cols)]
    prepare(2, "later")
    w_load.wait()

    def attended_step(p, _):
        rows = rows_at(p, group)
        attended_grad[rows, :] = jnp.dot(
            both[rows, :], wide[:, qkv_cols:], preferred_element_type=F32
        ).astype(BF)
        return 0

    for copy in arrays:
        copy.wait()
    lax.fori_loop(0, 2, attended_step, 0)
    branch.step(2)
    branch.step(3)
    outer.move(0, 0).wait_recv()
    rows_add(second, 2 * group, 2 * group, (got_core,))
    outer.move(1, 0).start()
    lax.fori_loop(2, 4, attended_step, 0)
    complete(2, "later")
    for p in range(4):
        branch.arrived(p)
    lax.fori_loop(4, 8, attended_step, 0)

    def outer_late():
        outer.move(1, 0).wait_recv()
        rows_add(second, group, group, (got_core, got_first))
        outer.move(2, 0).start()
        prepare(2, "total")

    def attention(table, aux, key_sum, value_sum):
        place.locate()
        table_load = pltpu.make_async_copy(table_out, table, load_sem.at[9])
        aux_load = pltpu.make_async_copy(aux_out, aux, load_sem.at[10])
        table_load.start()
        aux_load.start()
        table_load.wait()
        aux_load.wait()
        attend_back_blocks(
            place, q_ref, k_ref, v_ref, aux, marks_ref, attended_grad, table, qkv_grad, key_sum, value_sum,
            outer_late,
        )

    pl.run_scoped(
        attention,
        pltpu.VMEM((tokens, HEAD_SIZE), F32), pltpu.VMEM((tokens, HEAD_SIZE), F32),
        pltpu.VMEM((tokens, k_cols), F32), pltpu.VMEM((tokens, k_cols), F32),
    )
    place.locate()
    branch.sent()
    outer.move(2, 0).wait_recv()

    def output_step(rows):
        own_rows[rows, :] = (
            two[rows, :]
            + second[rows, :].astype(F32)
            + got_core[rows, :].astype(F32)
            + got_first[rows, :].astype(F32)
            + got_second[rows, :].astype(F32)
        ).astype(BF)

    by_rows(output_step)
    give_credit(1)
    blocks = HalfGather(place, own_rows, block_output, half_send.at[0], half_recv.at[0], load_sem.at[3])
    blocks.start()
    complete(2, "total")
    prepare(3, "first")

    def turn_rows(source, first, last):
        def step(b, _):
            rows = rows_at(b, group)
            turned[first:last, rows] = source[rows, :].T
            return 0

        lax.fori_loop(0, 8, step, 0)

    turn_rows(attended, qkv_cols, packed)
    weight_grads(SLICES, (qkv_cols,), (packed,), (both,))
    flush()
    sums[SLICES].start()
    normed_load = pltpu.make_async_copy(normed_out, both, load_sem.at[2])
    normed_load.start()
    complete(3, "first")
    turn_rows(qkv_grad, 0, qkv_cols)
    normed_load.wait()
    weight_grads(SLICES, (0,), (qkv_cols,), (both,))
    flush()
    sums[SLICES + 1].start()
    prepare(3, "later")

    outer.sent(0)
    pl.semaphore_wait(free_sem.at[1], 3)
    inner = PlaneSum(place, second, two, got, sum_send.at[3], sum_recv.at[3], chunk)
    for c in range(8):
        columns = pl.ds(c * chunk, chunk)

        def first_part(rows, c=c):
            return lax.dot_general(
                qkv_grad[rows, :], wide[c * chunk : (c + 1) * chunk, :qkv_cols], NT, preferred_element_type=F32
            )

        def first_rows(b, _, columns=columns, first_part=first_part):
            rows = rows_at(b, block)
            second[rows, columns] = first_part(rows).astype(BF)
            return 0

        first = first_part(pl.ds(0, block))
        two[:, columns] = first[:group]
        second[pl.ds(group, group), columns] = first[group:].astype(BF)
        lax.fori_loop(1, 4, first_rows, 0)
        inner.push(c)
        if c == 0:
            complete(3, "later")
        if c == 1:
            prepare(SLICES, "first")
        if c == 2:
            complete(SLICES, "first")
        if c == 4:
            prepare(SLICES + 1, "first")
        if c == 5:
            complete(SLICES + 1, "first")
        if c == 6:
            prepare(3, "total")
        if c == 7:
            complete(3, "total")
        if c >= 1:
            inner.middle(c - 1)
        if c >= 3:
            inner.late(c - 3)
        if c >= 5:
            inner.total(c - 5)
    inner.middle(7)
    prepare(SLICES, "later")
    blocks.step()
    for c in (5, 6, 7):
        inner.late(c)
        inner.total(c - 2)
    complete(SLICES, "later")
    inner.total(6)
    prepare(SLICES + 1, "later")
    inner.total(7)
    input_load = pltpu.make_async_copy(
        block_input.at[rows_at(place.tensor, group)], second.at[pl.ds(0, group)], load_sem.at[4]
    )
    input_load.start()
    input_load.wait()

    def first_step(rows):
        value, grad_first = second[rows, :].astype(F32), two[rows, :]
        factor = lax.rsqrt(jnp.mean(value * value, -1, keepdims=True) + EPS)
        normal = value * factor
        small_own[0:1, :] += jnp.sum(grad_first * normal, 0, keepdims=True)
        scaled = grad_first * gain_ref[0:1, :]
        input_grad = one[rows, :] + factor * (scaled - normal * jnp.mean(scaled * normal, -1, keepdims=True))
        second[rows, :] = input_grad.astype(BF)

    by_rows(first_step)
    gradients = HalfGather(
        place, second.at[pl.ds(0, group)], input_gradient, half_send.at[1], half_recv.at[1], load_sem.at[4]
    )
    gradients.start()
    complete(SLICES + 1, "later")

    for index, name in enumerate(("core", "y", "x")):
        move = place.copy(
            small_own.at[pl.ds(8 * index, 8)], small_got.at[index], small_send.at[index], small_recv.at[index], name
        )
        move.start()
        move.wait_recv()
        value = small_own[8 * index : 8 * index + 8, :] + small_got[index]
        if index < 2:
            small_own[8 * index + 8 : 8 * index + 16, :] = value
        else:
            small_all[place.sequence] = value
    gain_line = Line(place, lambda k: small_all.at[k], gain_send, gain_recv)
    gain_line.start(0)
    prepare(SLICES, "total")
    gradients.step()
    complete(SLICES, "total")
    for stage in range(count - 1):
        gain_line.arrived(stage)
        if stage < count - 2:
            gain_line.start(stage + 1)
    own_columns = pl.ds(pl.multiple_of(place.sequence * shard2, shard2), shard2)
    gain_out[...] = sum(small_all[k, :, own_columns] for k in range(count))
    prepare(SLICES + 1, "total")
    complete(SLICES + 1, "total")

    flush()
    for line in lines[1:]:
        for stage in range(count - 1):
            line.sent(stage)
    if gains_here:
        for stage in range(count - 1):
            gain_shards.sent(stage)
    for index in (1, 2, 3) if gains_here else (1, 2):
        early(index).wait_send()
    for item, item_sum in enumerate(sums):
        item_sum.sent(item == SLICES + 1)
    for arrived in swaps:
        arrived()
    for c in range(8):
        inner.sent(c)
    for index, name in enumerate(("core", "y", "x")):
        place.copy(
            small_own.at[pl.ds(8 * index, 8)], small_got.at[index], small_send.at[index], small_recv.at[index], name
        ).wait_send()
    for stage in range(count - 1):
        gain_line.sent(stage)
    blocks.end()
    gradients.end()


def rotation(table):
    other = pltpu.roll(table, HEAD_SIZE // 2, 1)
    low = lax.broadcasted_iota(jnp.int32, table.shape, 1) < HEAD_SIZE // 2
    return jnp.where(low, table, other), jnp.where(low, -other, table)


def attend_back_blocks(
    place, q_ref, k_ref, v_ref, aux, columns_ref, grad_ref, table, out_ref, key_sum, value_sum, late
):
    block = q_ref.shape[0] // 8
    scale = 1.0 / math.sqrt(HEAD_SIZE)
    q_cols, k_cols = q_ref.shape[1], k_ref.shape[1]
    key_sum[...] = jnp.zeros_like(key_sum)
    value_sum[...] = jnp.zeros_like(value_sum)
    for at in range(8):
        low, high = key_range(at, block)
        here = slice(at * block, high)
        span = slice(low, high)
        allowed = allowed_pairs(aux, columns_ref, at, block)
        keys, values = k_ref[span, :], v_ref[span, :]
        cosine, sine = rotation(table[here, :])
        to = rows_at(place.of_group(at), block)
        for head in range(q_cols // HEAD_SIZE):
            columns = slice(head * HEAD_SIZE, (head + 1) * HEAD_SIZE)
            rows = q_ref[here, columns]
            grad_rows = grad_ref[to, columns]
            scores = lax.dot_general(rows, keys, NT, preferred_element_type=F32) * scale
            scores = jnp.where(allowed, scores, NEGATIVE)
            probs = jnp.exp(scores - aux[here, 1 + head : 2 + head])
            value_sum[span, :] += lax.dot_general(
                probs.astype(BF), grad_rows, TN, preferred_element_type=F32
            )
            prob_grad = lax.dot_general(grad_rows, values, NT, preferred_element_type=F32)
            inner = jnp.sum(probs * prob_grad, -1, keepdims=True)
            score_grad = (probs * (prob_grad - inner)).astype(BF)
            query_grad = jnp.dot(score_grad, keys, preferred_element_type=F32) * scale
            key_sum[span, :] += lax.dot_general(score_grad, rows, TN, preferred_element_type=F32)
            out_ref[to, columns] = turn(query_grad, cosine, -sine).astype(BF)
        if at == 5:
            late()
    for at in range(8):
        here = slice(at * block, (at + 1) * block)
        cosine, sine = rotation(table[here, :])
        to = rows_at(place.of_group(at), block)
        out_ref[to, q_cols : q_cols + k_cols] = turn(key_sum[here, :] * scale, cosine, -sine).astype(BF)
        out_ref[to, q_cols + k_cols :] = value_sum[here, :].astype(BF)


def layer(block_input, out_grad, gains, table, marks, masters, count):
    half_tokens, width = block_input.shape
    group, tokens = half_tokens // 4, 2 * half_tokens
    shard = masters[0].shape[0]
    q_cols, k_cols = masters[0].shape[1] // 2, masters[1].shape[1] // 2
    slice_cols = masters[4].shape[1] // 2 // SLICES
    packed = 3 * slice_cols
    assert packed == 2 * q_cols + 2 * k_cols and q_cols == group >= shard
    gains_here = shard % 128 == 0
    if not gains_here:
        gains = lax.all_gather(gains, "dp", axis=1, tiled=True)
    part = shard if gains_here else 2 * shard
    vmem, hbm = pl.BlockSpec(memory_space=pltpu.VMEM), pl.BlockSpec(memory_space=pl.ANY)
    struct = jax.ShapeDtypeStruct
    dma = pltpu.SemaphoreType.DMA
    items = 1 + SLICES
    return pl.pallas_call(
        functools.partial(layer_kernel, count, gains_here),
        in_specs=[hbm, hbm, vmem, hbm, vmem] + [hbm] * 7,
        out_specs=[hbm] * 3 + [vmem] + [hbm] * 8,
        out_shape=[
            struct((half_tokens, width), BF),
            struct((half_tokens, width), BF),
            struct((2, items, packed, part), BF),
            struct((8, 2 * shard), F32),
            struct((items, packed, width), BF),
            struct((items, 2, count - 1, packed, 2 * shard), BF),
            struct((width, packed), BF),
            struct((SLICES, width, packed), BF),
            struct((tokens, width), BF),
            struct((tokens, packed), BF),
            struct((tokens, HEAD_SIZE), F32),
            struct((tokens, HEAD_SIZE), F32),
        ],
        scratch_shapes=[
            pltpu.VMEM((tokens, width), BF),
            pltpu.VMEM((tokens, width), BF),
            pltpu.VMEM((tokens, width), BF),
            pltpu.VMEM((width, packed), BF),
            pltpu.VMEM((4 * group, width), BF),
            pltpu.VMEM((2 * group, width), BF),
            pltpu.VMEM((group, width), BF),
            pltpu.VMEM((4, packed, 2 * shard), BF),
            pltpu.VMEM((count - 1, packed, 2 * shard), BF),
            pltpu.VMEM((2, packed, width // 4), BF),
            pltpu.VMEM((packed, tokens), BF),
            pltpu.VMEM((group, width), F32),
            pltpu.VMEM((group, width), F32),
            pltpu.VMEM((group, width), BF),
            pltpu.VMEM((24, width), F32),
            pltpu.VMEM((3, 8, width), F32),
            pltpu.VMEM((count, 8, width), F32),
            pltpu.VMEM((8, width), F32),
            pltpu.VMEM((8, tokens), F32),
            dma((12,)),
            dma((3 * SLICES,)),
            dma((2,)),
            dma((1 + items,)),
            dma((1 + items,)),
            dma((1 + items, 2, count - 1)),
            dma((1 + items, 2, count - 1)),
            dma((4, 3, 8)),
            dma((4, 3, 8)),
            dma((4, 7)),
            dma((4, 7)),
            dma((2, 3)),
            dma((2, 3)),
            dma((3,)),
            dma((3,)),
            dma((2, count - 1)),
            dma((2, count - 1)),
            pltpu.SemaphoreType.REGULAR((2,)),
            dma((4,)),
            dma((4,)),
            dma((4,)),
            dma((SLICES, 2)),
            dma((SLICES, 2)),
            dma((2 + items, 2, count - 1)),
            dma((2 + items, 2, count - 1)),
            dma((5,)),
            dma((SLICES, 2)),
            dma((4,)),
        ],
        compiler_params=pltpu.CompilerParams(
            vmem_limit_bytes=VMEM_LIMIT, collective_id=0, has_side_effects=True
        ),
        name="layer",
    )(block_input, out_grad, gains, table, marks, *masters)


def adamw(weight, gradient, first, second, rate, decay):
    first_new = BETA_ONE * first + (1.0 - BETA_ONE) * gradient
    second_new = BETA_TWO * second + (1.0 - BETA_TWO) * gradient * gradient
    bias_first = 1.0 - BETA_ONE**STEP
    bias_second = 1.0 - BETA_TWO**STEP
    moved = first_new * (1.0 / bias_first) / (jnp.sqrt(second_new * (1.0 / bias_second)) + ADAM_EPS)
    return (weight - rate * (moved + decay * weight), first_new, second_new)


def update_kernel(attention_cuts, forward_cuts, *refs):
    a, f = 12, 9
    attention_share, forward_share, block_in, gradient_in = refs[:4]
    states, outs = refs[4 : 4 + a + f], refs[4 + a + f :]
    outs[0][...] = block_in[...]
    outs[1][...] = gradient_in[...].astype(F32)

    def one(gradient, arrays, results, at):
        fresh = adamw(arrays[0][at], gradient, arrays[1][at], arrays[2][at], RATE_MATRIX, DECAY)
        for result, value in zip(results, fresh):
            result[at] = value

    everything = (slice(None), slice(None))
    for i in range(3):
        gradient = forward_share[forward_cuts[i] : forward_cuts[i + 1], :].astype(F32)
        one(gradient if i == 2 else gradient.T, states[a + i :: 3][:3], outs[2 + a + i :: 3][:3], everything)

    @pl.when(pl.program_id(0) == 0)
    def _():
        for i in range(4):
            for side in range(2):
                low, high = attention_cuts[i], attention_cuts[i + 1]
                gradient = attention_share[side, low:high, :].astype(F32)
                span = slice(side * (high - low), (side + 1) * (high - low))
                if i == 3:
                    one(gradient, states[i:a:4], outs[2 + i : 2 + a : 4], (span, slice(None)))
                else:
                    one(gradient.T, states[i:a:4], outs[2 + i : 2 + a : 4], (slice(None), span))


def update(shares, block_output, input_gradient, attention_cuts, attention, forward_cuts, feed):
    packed, part = shares.shape[2:]
    steps = 2 * SLICES

    def rows_block(array):
        return pl.BlockSpec((array.shape[0] // steps, array.shape[1]), lambda g: (g, 0))

    def columns_block(array):
        return pl.BlockSpec((array.shape[0], array.shape[1] // steps), lambda g: (0, g))

    state_specs = [pl.BlockSpec(array.shape, lambda g: (0, 0)) for array in attention]
    state_specs += [rows_block(array) if i % 3 == 2 else columns_block(array) for i, array in enumerate(feed)]
    plain = [rows_block(block_output), rows_block(input_gradient)]
    return pl.pallas_call(
        functools.partial(update_kernel, attention_cuts, forward_cuts),
        grid=(steps,),
        in_specs=[
            pl.BlockSpec((2, None, packed, part), lambda g: (0, SLICES, 0, 0)),
            pl.BlockSpec((None, None, packed, part), lambda g: (g // SLICES, g % SLICES, 0, 0)),
        ]
        + plain
        + state_specs,
        out_specs=plain + state_specs,
        out_shape=[
            jax.ShapeDtypeStruct(block_output.shape, BF),
            jax.ShapeDtypeStruct(input_gradient.shape, F32),
        ]
        + [jax.ShapeDtypeStruct(array.shape, F32) for array in (*attention, *feed)],
        compiler_params=pltpu.CompilerParams(vmem_limit_bytes=VMEM_LIMIT),
        name="update",
    )(shares, shares, block_output, input_gradient, *attention, *feed)


def rotary_tables(positions):
    half = HEAD_SIZE // 2
    frequency = THETA ** (-2.0 * jnp.arange(half, dtype=F32) / HEAD_SIZE)
    angles = positions.astype(F32)[:, None] * frequency[None, :]
    cosine, sine = jnp.cos(angles), jnp.sin(angles)
    return jnp.concatenate([cosine, sine], -1)


def local(
    block_input, out_grad, segments, positions,
    w_query, w_key, w_value, w_output, w_gate, w_up, w_down, gains,
    m_query, m_key, m_value, m_output, m_gate, m_up, m_down, m_gains,
    v_query, v_key, v_value, v_output, v_gate, v_up, v_down, v_gains,
):
    half_tokens = block_input.shape[0]
    rows = w_query.shape[0]
    sequences = lax.axis_size("dp") // 2
    half = lax.axis_index("dp") % 2
    table = rotary_tables(positions)
    marks = jnp.broadcast_to(segments.astype(F32)[None, :], (8, half_tokens))
    gain_rows = jnp.pad(gains.astype(BF).astype(F32), ((0, 6), (0, 0)))
    masters = (w_query, w_key, w_value, w_output, w_gate, w_up, w_down)
    block_output, input_gradient, shares, gain_grads = layer(
        block_input, out_grad, gain_rows, table, marks, masters, sequences
    )[:4]
    if shares.shape[-1] != rows:
        shares = lax.dynamic_slice_in_dim(shares, half * rows, rows, 3)
    q_cols, k_cols, o_cols = w_query.shape[1] // 2, w_key.shape[1] // 2, w_output.shape[0] // 2
    slice_cols = w_gate.shape[1] // 2 // SLICES

    def cuts(*sizes):
        return [sum(sizes[:i]) for i in range(len(sizes) + 1)]

    block_output, input_gradient, *fresh = update(
        shares, block_output, input_gradient,
        cuts(q_cols, k_cols, k_cols, o_cols),
        (w_query, w_key, w_value, w_output, m_query, m_key, m_value, m_output, v_query, v_key, v_value, v_output),
        cuts(slice_cols, slice_cols, slice_cols),
        (w_gate, w_up, w_down, m_gate, m_up, m_down, v_gate, v_up, v_down),
    )
    attention_new, forward_new = fresh[:12], fresh[12:]
    gain_grads = lax.dynamic_slice_in_dim(gain_grads[:2], half * rows, rows, 1)
    gains_new = adamw(gains, gain_grads, m_gains, v_gains, RATE_GAIN, 0.0)
    new = [
        list(attention_new[4 * part : 4 * part + 4]) + list(forward_new[3 * part : 3 * part + 3]) + [gains_new[part]]
        for part in range(3)
    ]
    return tuple([block_output, input_gradient] + new[0] + new[1] + new[2])


def solution(mesh):
    matrices = [P("dp", "tensor")] * 3 + [P("tensor", "dp")] + [P("dp", "tensor")] * 2 + [P("tensor", "dp")]
    state = tuple(matrices + [P(None, "dp")])
    rows = (P("dp", None), P("dp", None))
    return jax.shard_map(
        local,
        mesh=mesh,
        in_specs=rows + (P("dp"), P("dp")) + state * 3,
        out_specs=rows + state * 3,
        check_vma=False,
    )
```

time: 2580 us -> 637 us (0.25)
  waiting for transfers between devices: 2010 us -> 0 us
  Pallas kernels: 0 us -> 624 us
  matrix products: 295 us -> 0 us
  other arithmetic: 158 us -> 5.5 us
  local copies, waits for them, and re-layouts: 49.4 us -> 1.36 us
    reduce_scatter x7 -> x0, waiting for transfers between devices: 1090 us -> none  [the longest x1 284 us: local(): lax.psum_scatter(grad_w_gate, 'dp', scatter_dimension=0, tiled=True)]
    pallas_call x0 -> x2, Pallas kernels: none -> 624 us  [the longest x1 596 us: layer(): pl.pallas_call(functools.partial(layer_kernel, count, gains_here), in_spe...]
    psum x3 -> x0, waiting for transfers between devices: 422 us -> none  [the longest x1 144 us: local(): lax.psum(jnp.dot(attended, output_full, preferred_element_type=jnp.float3...]
    all_gather x7 -> x0, waiting for transfers between devices: 411 us -> none  [the longest x1 116 us: local(): lax.all_gather(w_gate.astype(jnp.bfloat16), 'dp', axis=0, tiled=True)]
    dot_general x35 -> x0, matrix products: 295 us -> none  [the longest x2 26.1 us: one_block(): jnp.einsum('qhgd,khd->hgqk', grad_rows, value_matrix, preferred_element_t...]
    convert_element_type x19 -> x3, other arithmetic: 67.6 us -> 1.39 us  [the longest x1 0.69 us: rotary_tables(): angles = positions.astype(F32)[:, None] * frequency[None, :]]
    unnamed x19 -> x0, waiting for transfers between devices: 49.2 us -> none
    ppermute x4 -> x0, waiting for transfers between devices: 35.3 us -> none  [passed_along(): return lax.ppermute(x, axis, pairs)]
  transfers between devices with their start and end apart: 22 -> 0, of which waited for: 20 -> 0; matrix products, arithmetic and copies ran while one was open for 11% -> 0% of each run, Pallas kernels for 0% -> 0%
where the time goes in v1:
time: 637 us; the launch traced here: 632 us
  Pallas kernels  624 us (98%)
    pallas_call x1, Pallas kernels, layer(): pl.pallas_call(functools.partial(layer_kernel, count, gains_here), in_spe...  596 us
    pallas_call x1, Pallas kernels, update(): pl.pallas_call(functools.partial(update_kernel, attention_cuts, forward_c...  28.1 us

profile of v1, /device:TPU:0, one launch (start us, length us, event | category | flops | bytes accessed | tf_op | source)
XLA Modules:
  0.0 632.3 jit_solution(15830682669577126062)
XLA Ops:
  0.7 0.0 copy-start.1
  0.7 0.7 convert_element_type.12
  1.4 0.6 pad_convert_fusion.gains
  2.0 0.7 convert_element_type.13
  2.7 1.9 multiply_cosine_fusion
  4.6 1.0 pad_maximum_fusion.table_half
  5.6 0.0 copy-done.1
  5.6 0.6 broadcast_in_dim.2.marks_half
  6.2 596.1 %layer.1 = (bf16[1024,2048]{1,0:T(8,128)(2,1)}, bf16[1024,2048]{1,0:T(8,128)(2,1)}, bf16[2,5,768,256]{3,2,1,0:T(8,128)(2,1)}, f32[8,512]{1,0:T(8,128)}, bf16[5,7...) custom-call(bf16[1024,2048]{1,0:T(8,128)(2,1)} %block_input.1, ...), custom_call_target="tpu_custom_call" | custom-call | tf_op jit(solution)/shard_map/layer/pallas_call | solution.py:1357
  602.3 0.0 copy-start
  602.3 0.0 copy-start.2
  602.4 0.0 copy-start.3
  602.4 28.1 %update.1 = (bf16[1024,2048]{1,0:T(8,128)(2,1)}, f32[1024,2048]{1,0:T(8,128)}, f32[256,512]{1,0:T(8,128)}, f32[256,256]{1,0:T(8,128)}, f32[256,256]{1,0:T(8,128)...) custom-call(bf16[2,5,768,256]{3,2,1,0:T(8,128)(2,1)} %get-tuple-elem, ...), custom_call_target="tpu_custom_call" | custom-call | tf_op jit(solution)/shard_map/update/pallas_call | solution.py:1483
  630.5 0.7 slice.3
  631.2 0.0 copy-done
  631.2 0.0 copy-done.2
  631.2 0.0 copy-done.3
  631.2 0.6 multiply_subtract_fusion
  (2 shorter events, 0.0 us)
Async XLA Ops:
  0.7 4.9 copy-start.1
  602.3 28.9 %copy-start = (f32[2,256]{1,0:T(2,128)S(1)}, f32[2,256]{1,0:T(2,128)}, u32[]{:S(2)}) copy-start(f32[2,256]{1,0:T(2,128)} %param.39) | copy-start | bytes 6148
  602.3 28.9 %copy-start.2 = (f32[2,256]{1,0:T(2,128)S(1)}, f32[2,256]{1,0:T(2,128)}, u32[]{:S(2)}) copy-start(f32[2,256]{1,0:T(2,128)} %param.47) | copy-start | bytes 6148
  602.4 28.9 %copy-start.3 = (f32[2,256]{1,0:T(2,128)S(1)}, f32[2,256]{1,0:T(2,128)}, u32[]{:S(2)}) copy-start(f32[2,256]{1,0:T(2,128)} %param.55) | copy-start | bytes 6148

commit v2 on v1

--- a/solution.py
+++ b/solution.py
@@ -434,12 +434,12 @@
     block_input, out_grad, gains, table_half, marks_half,
     w_query, w_key, w_value, w_output, w_gate, w_up, w_down,
     block_output, input_gradient, shares, gain_out,
-    own_grads, line_got, w_attention, w_forward, normed_out, heads_out, table_out, aux_out,
+    own_grads, line_got, totals, w_attention, w_forward, normed_out, heads_out, table_out, aux_out,
     second, grad, both, wide, got_core, got_first, got_second, loads, ring, ready, turned,
     one, two, own_rows, small_own, small_got, small_all, gain_ref, marks_ref,
     load_sem, wide_sem, ready_sem, swap_send, swap_recv, line_send, line_recv, sum_send, sum_recv,
     gather_send, gather_recv, half_send, half_recv, small_send, small_recv, gain_send, gain_recv, free_sem,
-    line_load_sem, early_send, early_recv, slice_send, slice_recv, shard_send, shard_recv, master_sem, keep_sem, out_sem,
+    line_load_sem, owner_sem, early_send, early_recv, slice_send, slice_recv, shard_send, shard_recv, master_sem, keep_sem, out_sem,
 ):
     place = Place(count)
     group, width = own_rows.shape
@@ -534,10 +534,10 @@
         place, lambda k: gain_ref.at[:, sequence_rows(k)], shard_send.at[1 + SLICES], shard_recv.at[1 + SLICES]
     )
 
-    begin = (0, 1, 2 * count - 3, 3 * count - 4)
+    begin = (0, 1, 2 * count - 4, 3 * count - 6.5)
     sends = sorted(
         ((s, stage) for s in range(SLICES) for stage in range(count - 1)),
-        key=lambda item: (begin[item[0]] + 2 * item[1], item[0]),
+        key=lambda item: (begin[item[0]] + 2 * item[1] + (item[1] > 0) * (item[0] >= 2) * 2, item[0]),
     )
 
     def advance(number):
@@ -746,7 +746,7 @@
                 grads.step(2)
             if c == 4:
                 grads.step(3)
-            if c == 6:
+            if c == 5:
                 advance(1)
         heads_copy.wait()
         aux_copy.wait()
@@ -757,7 +757,10 @@
     )
     place.locate()
     mixed.middle(7)
-    for c in (5, 6, 7):
+    mixed.late(5)
+    advance(1)
+    mixed.total(3)
+    for c in (6, 7):
         mixed.late(c)
         mixed.total(c - 2)
     mixed.total(6)
@@ -836,31 +839,38 @@
                 wait()
             pending[slot] = []
 
-    swaps = []
-
     def finish(index):
         item, low, size = sum_items[index]
         slot = next_ready()
         rows = pl.ds(low, size)
         sums[index].total(ready.at[slot, rows, pl.ds(0, shard2)])
 
-        def parts():
-            if part_width == shard2:
-                mine = theirs = ready.at[slot, rows, pl.ds(0, shard2)]
-            else:
-                mine, theirs = [
-                    ready.at[slot, rows, pl.ds(pl.multiple_of(side * part_width, part_width), part_width)]
-                    for side in (place.half, 1 - place.half)
-                ]
-            target = shares.at[place.half, item, rows]
-            keep = pltpu.make_async_copy(mine, target, ready_sem.at[slot])
-            swap = place.copy(theirs, target, swap_send.at[index], swap_recv.at[index], "x")
-            return keep, swap
-
-        for copy in parts():
+        def copy():
+            return pltpu.make_async_copy(
+                ready.at[slot, rows, pl.ds(0, shard2)], totals.at[item, rows], ready_sem.at[slot]
+            )
+
+        copy().start()
+        pending[slot].append(lambda: copy().wait())
+
+    def owner_moves(index):
+        item, low, size = sum_items[index]
+        rows = pl.ds(low, size)
+        if part_width == shard2:
+            mine = theirs = totals.at[item, rows]
+        else:
+            mine, theirs = [
+                totals.at[item, rows, pl.ds(pl.multiple_of(side * part_width, part_width), part_width)]
+                for side in (place.half, 1 - place.half)
+            ]
+        target = shares.at[place.half, item, rows]
+        keep = pltpu.make_async_copy(mine, target, owner_sem.at[index])
+        return keep, place.copy(theirs, target, swap_send.at[index], swap_recv.at[index], "x")
+
+    def to_owner(index):
+        flush()
+        for copy in owner_moves(index):
             copy.start()
-        pending[slot] += [lambda: parts()[0].wait(), lambda: parts()[1].wait_send()]
-        swaps.append(lambda: parts()[1].wait_recv())
 
     def stages_of(kind):
         return list(range(2, min(3, count)) if kind == "first" else range(3, count))
@@ -953,7 +963,7 @@
                     ((2, prepare, (0, "later")), (3, complete, (0, "later"))),
                     (
                         (0, prepare, (0, "total")), (1, complete, (0, "total")),
-                        (2, prepare, (1, "first")), (3, complete, (1, "first")),
+                        (2, prepare, (1, "first")), (3, complete, (1, "first")), (3, to_owner, (0,)),
                     ),
                 )[s],
             )
@@ -1127,21 +1137,6 @@
     )
     place.locate()
     branch.sent()
-    outer.move(2, 0).wait_recv()
-
-    def output_step(rows):
-        own_rows[rows, :] = (
-            two[rows, :]
-            + second[rows, :].astype(F32)
-            + got_core[rows, :].astype(F32)
-            + got_first[rows, :].astype(F32)
-            + got_second[rows, :].astype(F32)
-        ).astype(BF)
-
-    by_rows(output_step)
-    give_credit(1)
-    blocks = HalfGather(place, own_rows, block_output, half_send.at[0], half_recv.at[0], load_sem.at[3])
-    blocks.start()
     complete(2, "total")
     prepare(3, "first")
 
@@ -1165,6 +1160,23 @@
     weight_grads(SLICES, (0,), (qkv_cols,), (both,))
     flush()
     sums[SLICES + 1].start()
+    for index in (1, 2):
+        to_owner(index)
+    outer.move(2, 0).wait_recv()
+
+    def output_step(rows):
+        own_rows[rows, :] = (
+            two[rows, :]
+            + second[rows, :].astype(F32)
+            + got_core[rows, :].astype(F32)
+            + got_first[rows, :].astype(F32)
+            + got_second[rows, :].astype(F32)
+        ).astype(BF)
+
+    by_rows(output_step)
+    give_credit(1)
+    blocks = HalfGather(place, own_rows, block_output, half_send.at[0], half_recv.at[0], load_sem.at[3])
+    blocks.start()
     prepare(3, "later")
 
     outer.sent(0)
@@ -1209,6 +1221,7 @@
         if c >= 5:
             inner.total(c - 5)
     inner.middle(7)
+    to_owner(3)
     prepare(SLICES, "later")
     blocks.step()
     for c in (5, 6, 7):
@@ -1256,6 +1269,7 @@
     prepare(SLICES, "total")
     gradients.step()
     complete(SLICES, "total")
+    to_owner(SLICES)
     for stage in range(count - 1):
         gain_line.arrived(stage)
         if stage < count - 2:
@@ -1264,6 +1278,7 @@
     gain_out[...] = sum(small_all[k, :, own_columns] for k in range(count))
     prepare(SLICES + 1, "total")
     complete(SLICES + 1, "total")
+    to_owner(SLICES + 1)
 
     flush()
     for line in lines[1:]:
@@ -1276,8 +1291,10 @@
         early(index).wait_send()
     for item, item_sum in enumerate(sums):
         item_sum.sent(item == SLICES + 1)
-    for arrived in swaps:
-        arrived()
+    for index in range(len(sum_items)):
+        keep, swap = owner_moves(index)
+        keep.wait()
+        swap.wait()
     for c in range(8):
         inner.sent(c)
     for index, name in enumerate(("core", "y", "x")):
@@ -1357,7 +1374,7 @@
     return pl.pallas_call(
         functools.partial(layer_kernel, count, gains_here),
         in_specs=[hbm, hbm, vmem, hbm, vmem] + [hbm] * 7,
-        out_specs=[hbm] * 3 + [vmem] + [hbm] * 8,
+        out_specs=[hbm] * 3 + [vmem] + [hbm] * 9,
         out_shape=[
             struct((half_tokens, width), BF),
             struct((half_tokens, width), BF),
@@ -1365,6 +1382,7 @@
             struct((8, 2 * shard), F32),
             struct((items, packed, width), BF),
             struct((items, 2, count - 1, packed, 2 * shard), BF),
+            struct((items, packed, 2 * shard), BF),
             struct((width, packed), BF),
             struct((SLICES, width, packed), BF),
             struct((tokens, width), BF),
@@ -1411,6 +1429,7 @@
             dma((2, count - 1)),
             pltpu.SemaphoreType.REGULAR((2,)),
             dma((4,)),
+            dma((1 + items,)),
             dma((4,)),
             dma((4,)),
             dma((SLICES, 2)),

time: 637 us -> 621 us (0.975)
  Pallas kernels: 624 us -> 608 us
    pallas_call x1, Pallas kernels: 596 us -> 580 us  [layer(): pl.pallas_call(functools.partial(layer_kernel, count, gains_here), in_spe...]
where the time goes in v2:
time: 621 us; the launch traced here: 616 us
  Pallas kernels  608 us (98%)
    pallas_call x1, Pallas kernels, layer(): pl.pallas_call(functools.partial(layer_kernel, count, gains_here), in_spe...  580 us
    pallas_call x1, Pallas kernels, update(): pl.pallas_call(functools.partial(update_kernel, attention_cuts, forward_c...  28.1 us

profile of v2, /device:TPU:0, one launch (start us, length us, event | category | flops | bytes accessed | tf_op | source)
XLA Modules:
  0.0 616.1 jit_solution(75859824082590618)
XLA Ops:
  0.7 0.0 copy-start.1
  0.7 0.7 convert_element_type.12
  1.4 0.6 pad_convert_fusion.gains
  2.0 0.7 convert_element_type.13
  2.7 1.9 multiply_cosine_fusion
  4.6 1.0 pad_maximum_fusion.table_half
  5.6 0.0 copy-done.1
  5.6 0.6 broadcast_in_dim.2.marks_half
  6.2 580.0 %layer.1 = (bf16[1024,2048]{1,0:T(8,128)(2,1)}, bf16[1024,2048]{1,0:T(8,128)(2,1)}, bf16[2,5,768,256]{3,2,1,0:T(8,128)(2,1)}, f32[8,512]{1,0:T(8,128)}, bf16[5,7...) custom-call(bf16[1024,2048]{1,0:T(8,128)(2,1)} %block_input.1, ...), custom_call_target="tpu_custom_call" | custom-call | tf_op jit(solution)/shard_map/layer/pallas_call | solution.py:1374
  586.2 0.0 copy-start
  586.2 0.0 copy-start.2
  586.2 0.0 copy-start.3
  586.2 28.1 %update.1 = (bf16[1024,2048]{1,0:T(8,128)(2,1)}, f32[1024,2048]{1,0:T(8,128)}, f32[256,512]{1,0:T(8,128)}, f32[256,256]{1,0:T(8,128)}, f32[256,256]{1,0:T(8,128)...) custom-call(bf16[2,5,768,256]{3,2,1,0:T(8,128)(2,1)} %get-tuple-elem, ...), custom_call_target="tpu_custom_call" | custom-call | tf_op jit(solution)/shard_map/update/pallas_call | solution.py:1502
  614.3 0.7 slice.3
  615.1 0.0 copy-done
  615.1 0.0 copy-done.2
  615.1 0.0 copy-done.3
  615.1 0.6 multiply_subtract_fusion
  (2 shorter events, 0.0 us)
Async XLA Ops:
  0.7 4.9 copy-start.1
  586.2 28.9 %copy-start = (f32[2,256]{1,0:T(2,128)S(1)}, f32[2,256]{1,0:T(2,128)}, u32[]{:S(2)}) copy-start(f32[2,256]{1,0:T(2,128)} %param.39) | copy-start | bytes 6148
  586.2 28.9 %copy-start.2 = (f32[2,256]{1,0:T(2,128)S(1)}, f32[2,256]{1,0:T(2,128)}, u32[]{:S(2)}) copy-start(f32[2,256]{1,0:T(2,128)} %param.47) | copy-start | bytes 6148
  586.2 28.9 %copy-start.3 = (f32[2,256]{1,0:T(2,128)S(1)}, f32[2,256]{1,0:T(2,128)}, u32[]{:S(2)}) copy-start(f32[2,256]{1,0:T(2,128)} %param.55) | copy-start | bytes 6148

commit v3 on v2

--- a/solution.py
+++ b/solution.py
@@ -452,8 +452,7 @@
     qkv_cols = q_cols + 2 * k_cols
     shard2 = line_got.shape[-1]
     part_width = shares.shape[-1]
-    chunk = width // 8
-    big = width // 4
+    chunk = width // 4
     block = 2 * group
     got = (got_core, got_first, got_second)
 
@@ -715,7 +714,7 @@
         inputs.sent()
         normed_copy.wait()
 
-        for c in range(8):
+        for c in range(4):
             columns = pl.ds(c * chunk, chunk)
 
             def mixed_part(rows, c=c):
@@ -736,18 +735,16 @@
             mixed.push(c)
             if c >= 1:
                 mixed.middle(c - 1)
+            if c >= 2:
+                mixed.late(c - 2)
             if c >= 3:
-                mixed.late(c - 3)
-            if c >= 5:
-                mixed.total(c - 5)
+                mixed.total(c - 3)
+            if c == 1:
+                advance(1)
             if c == 2:
-                advance(1)
+                grads.step(2)
             if c == 3:
-                grads.step(2)
-            if c == 4:
                 grads.step(3)
-            if c == 5:
-                advance(1)
         heads_copy.wait()
         aux_copy.wait()
 
@@ -756,15 +753,13 @@
         pltpu.VMEM((tokens, packed), BF), pltpu.VMEM((tokens, HEAD_SIZE), F32), pltpu.VMEM((tokens, HEAD_SIZE), F32),
     )
     place.locate()
-    mixed.middle(7)
-    mixed.late(5)
+    mixed.middle(3)
     advance(1)
-    mixed.total(3)
-    for c in (6, 7):
-        mixed.late(c)
-        mixed.total(c - 2)
-    mixed.total(6)
-    mixed.total(7)
+    mixed.late(2)
+    mixed.late(3)
+    advance(1)
+    for c in (1, 2, 3):
+        mixed.total(c)
     early(0).wait_send()
 
     def by_rows(step):
@@ -793,7 +788,7 @@
     for stage in range(count - 1):
         lines[0].sent(stage)
         output_line.sent(stage)
-    for c in range(8):
+    for c in range(4):
         mixed.sent(c)
     for s in range(SLICES):
         for part in range(2):
@@ -890,21 +885,29 @@
                 sums[item].prepare(stage)
             sums[item].service(stage)
 
+    def weight_grads_chunk(item, low, high, right, c):
+        slot = next_ready()
+        columns = pl.ds(c * chunk, chunk)
+        for first, last, matrix in zip(low, high, right):
+            ready[slot, first:last, :] = jnp.dot(
+                turned[first:last, :], matrix[:, columns], preferred_element_type=F32
+            ).astype(BF)
+        rows = pl.ds(low[0], high[-1] - low[0])
+
+        def copy():
+            return pltpu.make_async_copy(
+                ready.at[slot, rows], own_grads.at[item, rows, columns], ready_sem.at[slot]
+            )
+
+        copy().start()
+        pending[slot].append(lambda: copy().wait())
+
     def weight_grads(item, low, high, right, tasks=()):
         for c in range(4):
             for at, do, task in tasks:
                 if at == c:
                     do(*task)
-            slot = next_ready()
-            columns = pl.ds(c * big, big)
-            for first, last, matrix in zip(low, high, right):
-                ready[slot, first:last, :] = jnp.dot(
-                    turned[first:last, :], matrix[:, columns], preferred_element_type=F32
-                ).astype(BF)
-            rows = pl.ds(low[0], high[-1] - low[0])
-            copy = pltpu.make_async_copy(ready.at[slot, rows], own_grads.at[item, rows, columns], ready_sem.at[slot])
-            copy.start()
-            pending[slot].append(copy.wait)
+            weight_grads_chunk(item, low, high, right, c)
 
     plane = PlaneSum(place, grad, one, got, sum_send.at[1], sum_recv.at[1], chunk)
 
@@ -971,44 +974,47 @@
             sums[s].start()
             advance(1)
 
-        def chunk_loads(c, low):
-            base = (c % 2) * SLICES
+        def held(c, s):
+            if c % 2 == 0:
+                return wide.at[pl.ds(s * chunk, chunk), pl.ds(0, pair)]
+            return turned.at[pl.ds(0, chunk), pl.ds(s * pair, pair)]
+
+        def held_branch(c, s):
+            return wide.at[pl.ds(s * chunk, chunk), pl.ds(pair if c % 2 == 0 else 0, slice_cols)]
+
+        def chunk_loads(c, where, low, size):
             return [
                 pltpu.make_async_copy(
-                    w_forward.at[s, pl.ds(c * chunk, chunk), pl.ds(low, packed - low)],
-                    wide.at[pl.ds((base + s) * chunk, chunk), pl.ds(low, packed - low)],
-                    wide_sem.at[SLICES + base + s],
+                    w_forward.at[s, pl.ds(c * chunk, chunk), pl.ds(low, size)], where(c, s),
+                    wide_sem.at[SLICES + (c % 2) * SLICES + s],
                 )
                 for s in range(SLICES)
             ]
 
-        def summed(source, rows, step, low, high, base):
+        def summed(source, rows, step, where, c):
             return sum(
                 lax.dot_general(
-                    source[rows, s * step : (s + 1) * step],
-                    wide[(base + s) * chunk : (base + s + 1) * chunk, low:high], NT,
-                    preferred_element_type=F32,
+                    source[rows, s * step : (s + 1) * step], where(c, s)[...], NT, preferred_element_type=F32
                 )
                 for s in range(SLICES)
             )
 
-        for copy in chunk_loads(0, 0):
+        for copy in chunk_loads(0, held, 0, pair):
             copy.start()
-        for c in range(8):
-            if c < 7:
-                for copy in chunk_loads(c + 1, 0):
+        for c in range(4):
+            if c < 3:
+                for copy in chunk_loads(c + 1, held, 0, pair):
                     copy.start()
-            for copy in chunk_loads(c, 0):
+            for copy in chunk_loads(c, held, 0, pair):
                 copy.wait()
-            base = (c % 2) * SLICES
             columns = pl.ds(c * chunk, chunk)
 
-            def grad_rows(b, _, columns=columns, base=base):
+            def grad_rows(b, _, columns=columns, c=c):
                 rows = rows_at(b, block)
-                grad[rows, columns] = summed(both, rows, pair, 0, pair, base).astype(BF)
+                grad[rows, columns] = summed(both, rows, pair, held, c).astype(BF)
                 return 0
 
-            first = summed(both, pl.ds(0, block), pair, 0, pair, base)
+            first = summed(both, pl.ds(0, block), pair, held, c)
             one[:, columns] = first[:group]
             grad[pl.ds(group, group), columns] = first[group:].astype(BF)
             lax.fori_loop(1, 4, grad_rows, 0)
@@ -1019,17 +1025,17 @@
                 plane.late(c - 2)
             if c >= 3:
                 plane.total(c - 3)
-            if c == 3:
+            if c == 1:
                 prepare(1, "later")
-            if c == 4:
+            if c == 2:
                 complete(1, "later")
-        for copy in chunk_loads(0, pair):
+        for copy in chunk_loads(0, held_branch, pair, slice_cols):
             copy.start()
-        plane.middle(7)
-        plane.late(6)
-        plane.late(7)
+        plane.middle(3)
+        plane.late(2)
+        plane.late(3)
         prepare(1, "total")
-        for c in (5, 6, 7):
+        for c in (1, 2, 3):
             plane.total(c)
         give_credit(0)
         complete(1, "total")
@@ -1037,24 +1043,24 @@
         by_rows(second_step)
         branch.start()
         prepare(2, "first")
-        for c in range(8):
-            if c < 7:
-                for copy in chunk_loads(c + 1, pair):
+        for c in range(4):
+            if c < 3:
+                for copy in chunk_loads(c + 1, held_branch, pair, slice_cols):
                     copy.start()
-            for copy in chunk_loads(c, pair):
+            for copy in chunk_loads(c, held_branch, pair, slice_cols):
                 copy.wait()
 
             def branch_rows(b, _, c=c):
                 rows = rows_at(b, block)
                 second[rows, pl.ds(c * chunk, chunk)] = summed(
-                    hidden, rows, slice_cols, pair, packed, (c % 2) * SLICES
+                    hidden, rows, slice_cols, held_branch, c
                 ).astype(BF)
                 return 0
 
             lax.fori_loop(0, 4, branch_rows, 0)
             if c == 0:
                 complete(2, "first")
-            if c == 5:
+            if c == 2:
                 branch.step(1)
 
     pl.run_scoped(feed_forward, pltpu.VMEM((tokens, SLICES * slice_cols), BF))
@@ -1078,7 +1084,7 @@
 
     pl.semaphore_wait(free_sem.at[0], 3)
     outer.push(0)
-    for c in range(8):
+    for c in range(4):
         plane.sent(c)
     marks = [0, q_cols, q_cols + k_cols, qkv_cols, qkv_cols + q_cols, qkv_cols + 2 * q_cols]
     arrays = [local(heads_out, grad.at[:, pl.ds(0, packed)], load_sem.at[5])]
@@ -1109,7 +1115,15 @@
     complete(2, "later")
     for p in range(4):
         branch.arrived(p)
-    lax.fori_loop(4, 8, attended_step, 0)
+
+    def attended_block(b, _):
+        rows = rows_at(b, block)
+        attended_grad[rows, :] = jnp.dot(
+            both[rows, :], wide[:, qkv_cols:], preferred_element_type=F32
+        ).astype(BF)
+        return 0
+
+    lax.fori_loop(2, 4, attended_block, 0)
 
     def outer_late():
         outer.move(1, 0).wait_recv()
@@ -1137,7 +1151,9 @@
     )
     place.locate()
     branch.sent()
+    to_owner(1)
     complete(2, "total")
+    to_owner(2)
     prepare(3, "first")
 
     def turn_rows(source, first, last):
@@ -1157,11 +1173,6 @@
     complete(3, "first")
     turn_rows(qkv_grad, 0, qkv_cols)
     normed_load.wait()
-    weight_grads(SLICES, (0,), (qkv_cols,), (both,))
-    flush()
-    sums[SLICES + 1].start()
-    for index in (1, 2):
-        to_owner(index)
     outer.move(2, 0).wait_recv()
 
     def output_step(rows):
@@ -1182,7 +1193,7 @@
     outer.sent(0)
     pl.semaphore_wait(free_sem.at[1], 3)
     inner = PlaneSum(place, second, two, got, sum_send.at[3], sum_recv.at[3], chunk)
-    for c in range(8):
+    for c in range(4):
         columns = pl.ds(c * chunk, chunk)
 
         def first_part(rows, c=c):
@@ -1206,31 +1217,23 @@
             prepare(SLICES, "first")
         if c == 2:
             complete(SLICES, "first")
-        if c == 4:
-            prepare(SLICES + 1, "first")
-        if c == 5:
-            complete(SLICES + 1, "first")
-        if c == 6:
-            prepare(3, "total")
-        if c == 7:
-            complete(3, "total")
+        weight_grads_chunk(SLICES, (0,), (qkv_cols,), (both,), c)
+        inner.middle(c)
         if c >= 1:
-            inner.middle(c - 1)
-        if c >= 3:
-            inner.late(c - 3)
-        if c >= 5:
-            inner.total(c - 5)
-    inner.middle(7)
-    to_owner(3)
+            inner.late(c - 1)
+        if c >= 2:
+            inner.total(c - 2)
+    flush()
+    sums[SLICES + 1].start()
+    prepare(3, "total")
+    inner.late(3)
+    complete(3, "total")
+    inner.total(2)
     prepare(SLICES, "later")
     blocks.step()
-    for c in (5, 6, 7):
-        inner.late(c)
-        inner.total(c - 2)
     complete(SLICES, "later")
-    inner.total(6)
-    prepare(SLICES + 1, "later")
-    inner.total(7)
+    inner.total(3)
+    to_owner(3)
     input_load = pltpu.make_async_copy(
         block_input.at[rows_at(place.tensor, group)], second.at[pl.ds(0, group)], load_sem.at[4]
     )
@@ -1247,11 +1250,12 @@
         second[rows, :] = input_grad.astype(BF)
 
     by_rows(first_step)
+    prepare(SLICES + 1, "first")
     gradients = HalfGather(
         place, second.at[pl.ds(0, group)], input_gradient, half_send.at[1], half_recv.at[1], load_sem.at[4]
     )
     gradients.start()
-    complete(SLICES + 1, "later")
+    complete(SLICES + 1, "first")
 
     for index, name in enumerate(("core", "y", "x")):
         move = place.copy(
@@ -1276,6 +1280,8 @@
             gain_line.start(stage + 1)
     own_columns = pl.ds(pl.multiple_of(place.sequence * shard2, shard2), shard2)
     gain_out[...] = sum(small_all[k, :, own_columns] for k in range(count))
+    prepare(SLICES + 1, "later")
+    complete(SLICES + 1, "later")
     prepare(SLICES + 1, "total")
     complete(SLICES + 1, "total")
     to_owner(SLICES + 1)
@@ -1295,7 +1301,7 @@
         keep, swap = owner_moves(index)
         keep.wait()
         swap.wait()
-    for c in range(8):
+    for c in range(4):
         inner.sent(c)
     for index, name in enumerate(("core", "y", "x")):
         place.copy(

time: 621 us -> 634 us (1.021)
  Pallas kernels: 608 us -> 618 us
    pallas_call x1, Pallas kernels: 580 us -> 590 us  [layer(): pl.pallas_call(functools.partial(layer_kernel, count, gains_here), in_spe...]
where the time goes in v3:
time: 634 us; the launch traced here: 626 us
  Pallas kernels  618 us (97%)
    pallas_call x1, Pallas kernels, layer(): pl.pallas_call(functools.partial(layer_kernel, count, gains_here), in_spe...  590 us
    pallas_call x1, Pallas kernels, update(): pl.pallas_call(functools.partial(update_kernel, attention_cuts, forward_c...  28.1 us

profile of v3, /device:TPU:0, one launch (start us, length us, event | category | flops | bytes accessed | tf_op | source)
XLA Modules:
  0.0 625.9 jit_solution(5605311492379686206)
XLA Ops:
  0.7 0.0 copy-start.1
  0.7 0.7 convert_element_type.12
  1.4 0.6 pad_convert_fusion.gains
  2.0 0.7 convert_element_type.13
  2.7 1.9 multiply_cosine_fusion
  4.6 1.0 pad_maximum_fusion.table_half
  5.6 0.0 copy-done.1
  5.6 0.6 broadcast_in_dim.2.marks_half
  6.2 589.7 %layer.1 = (bf16[1024,2048]{1,0:T(8,128)(2,1)}, bf16[1024,2048]{1,0:T(8,128)(2,1)}, bf16[2,5,768,256]{3,2,1,0:T(8,128)(2,1)}, f32[8,512]{1,0:T(8,128)}, bf16[5,7...) custom-call(bf16[1024,2048]{1,0:T(8,128)(2,1)} %block_input.1, ...), custom_call_target="tpu_custom_call" | custom-call | tf_op jit(solution)/shard_map/layer/pallas_call | solution.py:1380
  595.9 0.0 copy-start
  595.9 0.0 copy-start.2
  596.0 0.0 copy-start.3
  596.0 28.1 %update.1 = (bf16[1024,2048]{1,0:T(8,128)(2,1)}, f32[1024,2048]{1,0:T(8,128)}, f32[256,512]{1,0:T(8,128)}, f32[256,256]{1,0:T(8,128)}, f32[256,256]{1,0:T(8,128)...) custom-call(bf16[2,5,768,256]{3,2,1,0:T(8,128)(2,1)} %get-tuple-elem, ...), custom_call_target="tpu_custom_call" | custom-call | tf_op jit(solution)/shard_map/update/pallas_call | solution.py:1508
  624.1 0.7 slice.3
  624.8 0.0 copy-done
  624.8 0.0 copy-done.2
  624.8 0.0 copy-done.3
  624.8 0.6 multiply_subtract_fusion
  (2 shorter events, 0.0 us)
Async XLA Ops:
  0.7 4.9 copy-start.1
  595.9 28.9 %copy-start = (f32[2,256]{1,0:T(2,128)S(1)}, f32[2,256]{1,0:T(2,128)}, u32[]{:S(2)}) copy-start(f32[2,256]{1,0:T(2,128)} %param.39) | copy-start | bytes 6148
  595.9 28.9 %copy-start.2 = (f32[2,256]{1,0:T(2,128)S(1)}, f32[2,256]{1,0:T(2,128)}, u32[]{:S(2)}) copy-start(f32[2,256]{1,0:T(2,128)} %param.47) | copy-start | bytes 6148
  596.0 28.9 %copy-start.3 = (f32[2,256]{1,0:T(2,128)S(1)}, f32[2,256]{1,0:T(2,128)}, u32[]{:S(2)}) copy-start(f32[2,256]{1,0:T(2,128)} %param.55) | copy-start | bytes 6148

commit v4 on v2

--- a/solution.py
+++ b/solution.py
@@ -1137,7 +1137,9 @@
     )
     place.locate()
     branch.sent()
+    to_owner(1)
     complete(2, "total")
+    to_owner(2)
     prepare(3, "first")
 
     def turn_rows(source, first, last):
@@ -1160,8 +1162,6 @@
     weight_grads(SLICES, (0,), (qkv_cols,), (both,))
     flush()
     sums[SLICES + 1].start()
-    for index in (1, 2):
-        to_owner(index)
     outer.move(2, 0).wait_recv()
 
     def output_step(rows):
@@ -1211,9 +1211,9 @@
         if c == 5:
             complete(SLICES + 1, "first")
         if c == 6:
-            prepare(3, "total")
+            prepare(SLICES, "later")
         if c == 7:
-            complete(3, "total")
+            complete(SLICES, "later")
         if c >= 1:
             inner.middle(c - 1)
         if c >= 3:
@@ -1221,16 +1221,19 @@
         if c >= 5:
             inner.total(c - 5)
     inner.middle(7)
-    to_owner(3)
-    prepare(SLICES, "later")
+    prepare(SLICES + 1, "later")
     blocks.step()
-    for c in (5, 6, 7):
+    inner.late(5)
+    complete(SLICES + 1, "later")
+    inner.total(3)
+    for c in (6, 7):
         inner.late(c)
         inner.total(c - 2)
-    complete(SLICES, "later")
+    prepare(3, "total")
     inner.total(6)
-    prepare(SLICES + 1, "later")
     inner.total(7)
+    complete(3, "total")
+    to_owner(3)
     input_load = pltpu.make_async_copy(
         block_input.at[rows_at(place.tensor, group)], second.at[pl.ds(0, group)], load_sem.at[4]
     )
@@ -1251,34 +1254,41 @@
         place, second.at[pl.ds(0, group)], input_gradient, half_send.at[1], half_recv.at[1], load_sem.at[4]
     )
     gradients.start()
-    complete(SLICES + 1, "later")
-
-    for index, name in enumerate(("core", "y", "x")):
-        move = place.copy(
-            small_own.at[pl.ds(8 * index, 8)], small_got.at[index], small_send.at[index], small_recv.at[index], name
+
+    def small_move(index):
+        return place.copy(
+            small_own.at[pl.ds(8 * index, 8)], small_got.at[index], small_send.at[index], small_recv.at[index],
+            ("core", "y", "x")[index],
         )
-        move.start()
-        move.wait_recv()
+
+    def small_sum(index):
+        small_move(index).wait_recv()
         value = small_own[8 * index : 8 * index + 8, :] + small_got[index]
         if index < 2:
             small_own[8 * index + 8 : 8 * index + 16, :] = value
+            small_move(index + 1).start()
         else:
             small_all[place.sequence] = value
+
+    small_move(0).start()
+    prepare(SLICES, "total")
+    small_sum(0)
+    complete(SLICES, "total")
+    to_owner(SLICES)
+    small_sum(1)
+    prepare(SLICES + 1, "total")
+    small_sum(2)
     gain_line = Line(place, lambda k: small_all.at[k], gain_send, gain_recv)
     gain_line.start(0)
-    prepare(SLICES, "total")
+    complete(SLICES + 1, "total")
+    to_owner(SLICES + 1)
     gradients.step()
-    complete(SLICES, "total")
-    to_owner(SLICES)
     for stage in range(count - 1):
         gain_line.arrived(stage)
         if stage < count - 2:
             gain_line.start(stage + 1)
     own_columns = pl.ds(pl.multiple_of(place.sequence * shard2, shard2), shard2)
     gain_out[...] = sum(small_all[k, :, own_columns] for k in range(count))
-    prepare(SLICES + 1, "total")
-    complete(SLICES + 1, "total")
-    to_owner(SLICES + 1)
 
     flush()
     for line in lines[1:]:
@@ -1297,10 +1307,8 @@
         swap.wait()
     for c in range(8):
         inner.sent(c)
-    for index, name in enumerate(("core", "y", "x")):
-        place.copy(
-            small_own.at[pl.ds(8 * index, 8)], small_got.at[index], small_send.at[index], small_recv.at[index], name
-        ).wait_send()
+    for index in range(3):
+        small_move(index).wait_send()
     for stage in range(count - 1):
         gain_line.sent(stage)
     blocks.end()

time: 621 us -> 610 us (0.982)
  Pallas kernels: 608 us -> 593 us
    pallas_call x1, Pallas kernels: 580 us -> 565 us  [layer(): pl.pallas_call(functools.partial(layer_kernel, count, gains_here), in_spe...]
where the time goes in v4:
time: 610 us; the launch traced here: 601 us
  Pallas kernels  593 us (97%)
    pallas_call x1, Pallas kernels, layer(): pl.pallas_call(functools.partial(layer_kernel, count, gains_here), in_spe...  565 us
    pallas_call x1, Pallas kernels, update(): pl.pallas_call(functools.partial(update_kernel, attention_cuts, forward_c...  28.1 us

profile of v4, /device:TPU:0, one launch (start us, length us, event | category | flops | bytes accessed | tf_op | source)
XLA Modules:
  0.0 601.3 jit_solution(1227901283807951657)
XLA Ops:
  0.7 0.0 copy-start.1
  0.7 0.7 convert_element_type.12
  1.4 0.6 pad_convert_fusion.gains
  2.0 0.7 convert_element_type.13
  2.7 1.9 multiply_cosine_fusion
  4.6 1.0 pad_maximum_fusion.table_half
  5.6 0.0 copy-done.1
  5.6 0.6 broadcast_in_dim.2.marks_half
  6.2 565.2 %layer.1 = (bf16[1024,2048]{1,0:T(8,128)(2,1)}, bf16[1024,2048]{1,0:T(8,128)(2,1)}, bf16[2,5,768,256]{3,2,1,0:T(8,128)(2,1)}, f32[8,512]{1,0:T(8,128)}, bf16[5,7...) custom-call(bf16[1024,2048]{1,0:T(8,128)(2,1)} %block_input.1, ...), custom_call_target="tpu_custom_call" | custom-call | tf_op jit(solution)/shard_map/layer/pallas_call | solution.py:1382
  571.4 0.0 copy-start
  571.4 0.0 copy-start.2
  571.4 0.0 copy-start.3
  571.4 28.1 %update.1 = (bf16[1024,2048]{1,0:T(8,128)(2,1)}, f32[1024,2048]{1,0:T(8,128)}, f32[256,512]{1,0:T(8,128)}, f32[256,256]{1,0:T(8,128)}, f32[256,256]{1,0:T(8,128)...) custom-call(bf16[2,5,768,256]{3,2,1,0:T(8,128)(2,1)} %get-tuple-elem, ...), custom_call_target="tpu_custom_call" | custom-call | tf_op jit(solution)/shard_map/update/pallas_call | solution.py:1510
  599.6 0.7 slice.3
  600.3 0.0 copy-done
  600.3 0.0 copy-done.2
  600.3 0.0 copy-done.3
  600.3 0.6 multiply_subtract_fusion
  (2 shorter events, 0.0 us)
Async XLA Ops:
  0.7 4.9 copy-start.1
  571.4 28.9 %copy-start = (f32[2,256]{1,0:T(2,128)S(1)}, f32[2,256]{1,0:T(2,128)}, u32[]{:S(2)}) copy-start(f32[2,256]{1,0:T(2,128)} %param.39) | copy-start | bytes 6148
  571.4 28.9 %copy-start.2 = (f32[2,256]{1,0:T(2,128)S(1)}, f32[2,256]{1,0:T(2,128)}, u32[]{:S(2)}) copy-start(f32[2,256]{1,0:T(2,128)} %param.47) | copy-start | bytes 6148
  571.4 28.9 %copy-start.3 = (f32[2,256]{1,0:T(2,128)S(1)}, f32[2,256]{1,0:T(2,128)}, u32[]{:S(2)}) copy-start(f32[2,256]{1,0:T(2,128)} %param.55) | copy-start | bytes 6148
